TPU v7x, 32 devices: a whole 2x2x4 slice. The times are simulated.
32 devices in a mesh: groups: 2 (over y), rows: 4 (over z), shard: 4 (over x, core).
Axes of the slice: x: 2, y: 2, z: 4, core: 2. Of those that a mesh axis runs over, the one named last changes fastest.
Arguments:
- images: bfloat16 [8, 8, 128, 512], P(('groups', 'shard'), 'rows'), parts along dimension 0, may hold values from -6 to 6
- cotangent: bfloat16 [8, 8, 128, 512], P(('groups', 'shard'), 'rows'), parts along dimension 0, may hold values from -6 to 6
- weight_in: bfloat16 [2, 512, 512], P(None, 'shard'), may hold values from -0.25 to 0.25
- weight_group: bfloat16 [2, 144, 512], P(None, 'shard'), may hold values from -0.5 to 0.5
- weight_out: bfloat16 [2, 512, 512], P(None, 'shard'), may hold values from -0.25 to 0.25
Outputs:
- decoded: bfloat16 [8, 8, 128, 512], P(('groups', 'shard'), 'rows'), parts along dimension 0
- grad_images: bfloat16 [8, 8, 128, 512], P(('groups', 'shard'), 'rows'), parts along dimension 0
- grad_in: float32 [4, 512, 512], P('groups', 'shard'), parts along dimension 0
- grad_group: float32 [4, 144, 512], P('groups', 'shard'), parts along dimension 0
- grad_out: float32 [4, 512, 512], P('groups', 'shard'), parts along dimension 0
There are 2 independent parts, one for each index of `groups`. A program takes and returns all parts, laid end to end along the dimension named above; an argument that names none is the same for every part. Nothing has to cross between parts.
All inputs are finite; a program needn't handle non-finite values.
Results may differ from a plain program's by a relative error of at most 0.02.
Values may be sent and summed in bfloat16 or wider, within the bound.
A program may use at most 128 MiB of HBM per device.

v0:
```python
import math

import jax
import jax.numpy as jnp
from jax import lax
from jax.sharding import PartitionSpec as P

GW = 16


def extended_2(cells, sides, width):
    for axis, dim in sides:
        count = lax.axis_size(axis)
        ends = count - 1
        head = lax.slice_in_dim(cells, 0, width, axis=dim)
        tail = lax.slice_in_dim(cells, cells.shape[dim] - width, cells.shape[dim], axis=dim)
        cells = jnp.concatenate(
            [
                lax.ppermute(tail, axis, [(i, (i + 1) % count) for i in range(ends)]),
                cells,
                lax.ppermute(head, axis, [((i + 1) % count, i) for i in range(ends)]),
            ],
            axis=dim,
        )
    return cells


def silu_slope(preact):
    sigmoid_value = jax.nn.sigmoid(preact)
    return sigmoid_value * (1.0 + preact * (1.0 - sigmoid_value))


def block_kernel(full_group, hidden_width, group_width):
    sub_width = min(hidden_width, 128)
    sections = hidden_width // sub_width
    members = sub_width // group_width
    arranged = full_group.reshape(9, group_width, sections, members, group_width)
    arranged = arranged.transpose(0, 2, 3, 1, 4)
    identity = jnp.eye(members, dtype=full_group.dtype)
    expanded = arranged[:, :, :, :, None, :] * identity[None, None, :, None, :, None]
    return expanded.reshape(9, sections, sub_width, sub_width)


def grouped_taps(padded, kernel, out_rows, out_cols, flipped, pattern):
    summed = None
    for tap_index in range(9):
        row_step = tap_index // 3
        col_step = tap_index % 3
        if flipped:
            row_step = 2 - row_step
            col_step = 2 - col_step
        window = padded[:, row_step : row_step + out_rows, col_step : col_step + out_cols, :]
        window = window.reshape(-1, kernel.shape[1], kernel.shape[2])
        tap_term = jnp.einsum(
            pattern, window, kernel[tap_index], preferred_element_type=jnp.float32
        )
        summed = tap_term if summed is None else summed + tap_term
    return summed


def body(images, cotangent, weight_in, weight_group, weight_out):
    tile_count, height, across, channels = images.shape
    block_count = weight_in.shape[0]
    group_width = GW
    pixels = tile_count * height * across
    current = images.reshape(pixels, channels)
    stored = []
    for block_index in range(block_count):
        full_in, full_group, full_out = (
            lax.all_gather(weight_in[block_index], "shard", axis=0, tiled=True),
            lax.all_gather(weight_group[block_index], "shard", axis=0, tiled=True),
            lax.all_gather(weight_out[block_index], "shard", axis=0, tiled=True),
        )
        hidden_width = full_in.shape[1]
        kernel = block_kernel(full_group, hidden_width, group_width)
        pre_one = jnp.dot(current, full_in, preferred_element_type=jnp.float32)
        hidden_one = (
            jax.nn.silu(pre_one)
            .astype(jnp.bfloat16)
            .reshape(tile_count, height, across, hidden_width)
        )
        haloed = extended_2(hidden_one, (("rows", 1),), 1)
        padded_one = jnp.pad(haloed, ((0, 0), (0, 0), (1, 1), (0, 0)))
        pre_two = grouped_taps(padded_one, kernel, height, across, False, "psi,sio->pso").reshape(
            pixels, hidden_width
        )
        hidden_two = jax.nn.silu(pre_two).astype(jnp.bfloat16)
        pre_three = current.astype(jnp.float32) + jnp.dot(
            hidden_two, full_out, preferred_element_type=jnp.float32
        )
        kept_weights = None
        stored.append((current, pre_one, padded_one, pre_two, hidden_two, pre_three, kept_weights))
        current = jax.nn.silu(pre_three).astype(jnp.bfloat16)
    decoded = current.reshape(images.shape)
    grad_flow = cotangent.reshape(pixels, channels)
    shares = []
    for block_index in reversed(range(block_count)):
        flow_in, pre_one, padded_one, pre_two, hidden_two, pre_three, kept_weights = stored[
            block_index
        ]
        full_in, full_group, full_out = (
            lax.all_gather(weight_in[block_index], "shard", axis=0, tiled=True),
            lax.all_gather(weight_group[block_index], "shard", axis=0, tiled=True),
            lax.all_gather(weight_out[block_index], "shard", axis=0, tiled=True),
        )
        hidden_width = full_in.shape[1]
        kernel = block_kernel(full_group, hidden_width, group_width)
        sections = kernel.shape[1]
        sub_width = kernel.shape[2]
        members = sub_width // group_width
        slope_three = grad_flow.astype(jnp.float32) * silu_slope(pre_three)
        low_three = slope_three.astype(jnp.bfloat16)
        part_out = jnp.einsum(
            "pw,pc->wc", hidden_two, low_three, preferred_element_type=jnp.float32
        )
        slope_two = (
            jnp.einsum("pc,wc->pw", low_three, full_out, preferred_element_type=jnp.float32)
            * silu_slope(pre_two)
        ).astype(jnp.bfloat16)
        slope_sections = slope_two.reshape(pixels, sections, sub_width)
        tap_terms = []
        for tap_index in range(9):
            row_step = tap_index // 3
            col_step = tap_index % 3
            window = padded_one[:, row_step : row_step + height, col_step : col_step + across, :]
            window = window.reshape(pixels, sections, sub_width)
            blockwise = jnp.einsum(
                "psi,pso->sio", window, slope_sections, preferred_element_type=jnp.float32
            )
            blockwise = blockwise.reshape(sections, members, group_width, members, group_width)
            diagonal_part = jnp.diagonal(blockwise, axis1=1, axis2=3)
            tap_terms.append(diagonal_part.transpose(1, 0, 3, 2).reshape(group_width, hidden_width))
        part_group = jnp.stack(tap_terms).reshape(9 * group_width, hidden_width)
        slope_grid = slope_two.reshape(tile_count, height, across, hidden_width)
        padded_slope = jnp.pad(slope_grid, ((0, 0), (2, 2), (1, 1), (0, 0)))
        extended = grouped_taps(padded_slope, kernel, height + 2, across, True, "pso,sio->psi")
        extended = extended.reshape(tile_count, height + 2, across, hidden_width)
        edge_rows = jnp.concatenate([extended[:, :1], extended[:, -1:]], axis=1)
        borders = extended_2(edge_rows.astype(jnp.bfloat16), (("rows", 1),), 1).astype(
            edge_rows.dtype
        )
        back_one = extended[:, 1:-1]
        back_one = back_one.at[:, :1].add(borders[:, :1])
        back_one = back_one.at[:, -1:].add(borders[:, -1:])
        slope_one = (back_one.reshape(pixels, hidden_width) * silu_slope(pre_one)).astype(
            jnp.bfloat16
        )
        part_in = jnp.einsum("pc,pw->cw", flow_in, slope_one, preferred_element_type=jnp.float32)
        grad_flow = (
            slope_three
            + jnp.einsum("pw,cw->pc", slope_one, full_in, preferred_element_type=jnp.float32)
        ).astype(jnp.bfloat16)
        shares.append(
            (
                lax.psum_scatter(
                    part_in.astype(jnp.bfloat16), "shard", scatter_dimension=0, tiled=True
                ).astype(jnp.float32),
                lax.psum_scatter(
                    part_group.astype(jnp.bfloat16), "shard", scatter_dimension=0, tiled=True
                ).astype(jnp.float32),
                lax.psum_scatter(
                    part_out.astype(jnp.bfloat16), "shard", scatter_dimension=0, tiled=True
                ).astype(jnp.float32),
            )
        )
    shares = shares[::-1]
    totals = (
        lax.psum(jnp.stack([entry[0] for entry in shares]).astype(jnp.bfloat16), "rows").astype(
            jnp.float32
        ),
        lax.psum(jnp.stack([entry[1] for entry in shares]).astype(jnp.bfloat16), "rows").astype(
            jnp.float32
        ),
        lax.psum(jnp.stack([entry[2] for entry in shares]).astype(jnp.bfloat16), "rows").astype(
            jnp.float32
        ),
    )
    norm_factor = 1.0 / math.sqrt(pixels * lax.axis_size("rows") * lax.axis_size("shard"))
    grad_images = grad_flow.reshape(images.shape)
    return (
        decoded,
        grad_images,
        totals[0] * norm_factor,
        totals[1] * norm_factor,
        totals[2] * norm_factor,
    )


def solution(mesh):
    placed = (
        P(("groups", "shard"), "rows", None, None),
        P(("groups", "shard"), "rows", None, None),
        P(None, "shard", None),
        P(None, "shard", None),
        P(None, "shard", None),
    )
    return jax.shard_map(
        body,
        mesh=mesh,
        in_specs=placed,
        out_specs=(
            P(("groups", "shard"), "rows", None, None),
            P(("groups", "shard"), "rows", None, None),
            P("groups", "shard", None),
            P("groups", "shard", None),
            P("groups", "shard", None),
        ),
        check_vma=False,
    )
```

profile of v0, /device:TPU:0, one launch (start us, length us, event | category | flops | bytes accessed | tf_op | source)
XLA Modules:
  0.0 434.6 jit_solution(18209110213923368101)
XLA Ops:
  8.9 8.6 %all-gather.1 = bf16[1,512,512]{2,1,0:T(8,128)(2,1)S(1)} all-gather(bf16[1,128,512]{2,1,0:T(8,128)(2,1)S(1)} %get-tuple-element.137), channel_id=3, replica_groups=mesh['groups'=2,'rows'=4,'shard'=4] {'shard'}, dimensions={1}, use_global_device_ids=true | all-gather | bytes 655360 | tf_op jit(solution)/shard_map/all_gather | solution.py:70
  20.6 5.2 %collective-permute-start = (bf16[1,1,128,512]{3,2,1,0:T(8,128)(2,1)}, bf16[1,1,128,512]{3,2,1,0:T(8,128)(2,1)}, u32[]{:S(2)}, u32[]{:S(2)}) collective-permute-start(bf16[1,1,128,512]{3,2,1,0:T(8,128)(2,1)} %get-tuple-element.135), channel_id=1, source_target_pairs={{0,4},{4,8},{8,12},{1,5},{5,9},{9,13},{2,6},{6,10},{10,14},{3,7},{... | collective-permute-start | bytes 393224 | tf_op jit(solution)/shard_map/ppermute | solution.py:19
  27.5 5.9 %all-gather = bf16[1,144,512]{2,0,1:T(2,128)(2,1)S(1)} all-gather(bf16[1,36,512]{2,0,1:T(2,128)(2,1)S(1)} %get-tuple-element.141), channel_id=2, replica_groups=mesh['groups'=2,'rows'=4,'shard'=4] {'shard'}, dimensions={1}, use_global_device_ids=true | all-gather | bytes 184320 | tf_op jit(solution)/shard_map/all_gather | solution.py:71
  36.6 6.0 %all-gather.3 = bf16[1,144,512]{2,0,1:T(2,128)(2,1)S(1)} all-gather(bf16[1,36,512]{2,0,1:T(2,128)(2,1)S(1)} %get-tuple-element.142), channel_id=5, replica_groups=mesh['groups'=2,'rows'=4,'shard'=4] {'shard'}, dimensions={1}, use_global_device_ids=true | all-gather | bytes 184320 | tf_op jit(solution)/shard_map/all_gather | solution.py:71
  45.9 9.0 %all-gather.4 = bf16[1,512,512]{2,1,0:T(8,128)(2,1)} all-gather(bf16[1,128,512]{2,1,0:T(8,128)(2,1)} %get-tuple-element.138), channel_id=6, replica_groups=mesh['groups'=2,'rows'=4,'shard'=4] {'shard'}, dimensions={1}, use_global_device_ids=true | all-gather | bytes 655360 | tf_op jit(solution)/shard_map/all_gather | solution.py:70
  54.9 4.4 %broadcast_multiply_fusion.1 = (bf16[9,4,8,16,8,16]{3,2,5,4,1,0:T(8,128)(2,1)S(1)}, bf16[9,4,8,16,8,16]{3,2,5,4,1,0:T(8,128)(2,1)}) fusion(bf16[8,8]{0,1:T(8,128)(2,1)S(1)} %fusion.107, bf16[9,4,8,16,16]{3,2,4,1,0:T(8,128)(2,1)S(1)} %copy.227, bf16[9,4,8,16,16]{3,2,4,1,0:T(8,128)(2,1)S(1)} %copy.238), kind=kLoop, calls=%fused_computation.19 | loop fusion | flops 1179648 | bytes 2654336 | tf_op jit(solution)/shard_map/mul | solution.py:40
  59.3 9.0 %fusion.109 = (bf16[1,4,8,16,8,16]{3,2,5,4,1,0:T(8,128)(2,1)S(1)}, bf16[1,4,8,16,8,16]{3,2,5,4,1,0:T(8,128)(2,1)S(1)}, bf16[1,4,8,16,8,16]{3,2,5,4,1,0:T(8,128)(...) fusion(bf16[9,4,8,16,8,16]{3,2,5,4,1,0:T(8,128)(2,1)} %get-tupl, ...), kind=kLoop, calls=%fused_computation.285 | loop fusion | bytes 4718592 | tf_op jit(solution)/shard_map/slice | solution.py:55
  68.3 2.0 squeeze.97
  70.3 2.6 squeeze.99
  73.0 2.6 squeeze.100
  75.6 2.6 squeeze.101
  78.2 2.6 squeeze.102
  80.8 2.6 squeeze.103
  83.4 2.6 squeeze.104
  86.0 2.6 squeeze.105
  88.6 2.6 squeeze.106
  91.2 8.9 %all-gather.2 = bf16[1,512,512]{2,1,0:T(8,128)(2,1)} all-gather(bf16[1,128,512]{2,1,0:T(8,128)(2,1)} %get-tuple-element.139), channel_id=4, replica_groups=mesh['groups'=2,'rows'=4,'shard'=4] {'shard'}, dimensions={1}, use_global_device_ids=true | all-gather | bytes 655360 | tf_op jit(solution)/shard_map/all_gather | solution.py:72
  104.1 1.8 copy.294
  105.9 1.8 pad_maximum_fusion.2
  115.7 1.8 copy.306
  121.8 1.8 copy.318
  125.4 1.8 copy.322
  136.4 2.1 copy.389
  143.2 5.2 %collective-permute-start.2 = (bf16[1,1,128,512]{3,2,1,0:T(8,128)(2,1)}, bf16[1,1,128,512]{3,2,1,0:T(8,128)(2,1)}, u32[]{:S(2)}, u32[]{:S(2)}) collective-permute-start(bf16[1,1,128,512]{3,2,1,0:T(8,128)(2,1)} %get-tuple-element.131), channel_id=1, source_target_pairs={{0,4},{4,8},{8,12},{1,5},{5,9},{9,13},{2,6},{6,10},{10,14},{3,7},{... | collective-permute-start | bytes 393224 | tf_op jit(solution)/shard_map/ppermute | solution.py:19
  148.4 7.2 %all-gather.5 = bf16[1,512,512]{2,1,0:T(8,128)(2,1)} all-gather(bf16[1,128,512]{2,1,0:T(8,128)(2,1)S(1)} %copy-done.92), channel_id=7, replica_groups=mesh['groups'=2,'rows'=4,'shard'=4] {'shard'}, dimensions={1}, use_global_device_ids=true | all-gather | bytes 655360 | tf_op jit(solution)/shard_map/all_gather | solution.py:72
  155.7 2.6 squeeze.109
  158.3 2.6 squeeze.111
  160.9 2.6 squeeze.112
  163.5 2.6 squeeze.113
  166.1 2.6 squeeze.114
  168.7 3.0 squeeze.115
  186.1 2.7 convert_multiply_fusion
  202.2 2.0 reshape.650
  204.2 2.0 reshape.651
  206.2 2.0 reshape.652
  208.1 1.9 reshape.653
  223.4 5.2 %collective-permute-start.4 = (bf16[1,1,128,512]{3,2,1,0:T(8,128)(2,1)}, bf16[1,1,128,512]{3,2,1,0:T(8,128)(2,1)}, u32[]{:S(2)}, u32[]{:S(2)}) collective-permute-start(bf16[1,1,128,512]{3,2,1,0:T(8,128)(2,1)} %copy.401), channel_id=1, source_target_pairs={{0,4},{4,8},{8,12},{1,5},{5,9},{9,13},{2,6},{6,10},{10,14},{3,7},{... | collective-permute-start | bytes 393224 | tf_op jit(solution)/shard_map/ppermute | solution.py:19
  268.0 2.0 reshape.662
  270.0 2.0 reshape.663
  272.0 2.0 reshape.664
  274.0 2.0 reshape.665
  291.3 5.4 %collective-permute-start.6 = (bf16[1,1,128,512]{3,2,1,0:T(8,128)(2,1)}, bf16[1,1,128,512]{3,2,1,0:T(8,128)(2,1)}, u32[]{:S(2)}, u32[]{:S(2)}) collective-permute-start(bf16[1,1,128,512]{3,2,1,0:T(8,128)(2,1)} %copy.405), channel_id=1, source_target_pairs={{0,4},{4,8},{8,12},{1,5},{5,9},{9,13},{2,6},{6,10},{10,14},{3,7},{... | collective-permute-start | bytes 393224 | tf_op jit(solution)/shard_map/ppermute | solution.py:19
  307.8 2.3 convolution_convert_fusion.2
  330.1 8.7 %fusion.108 = (bf16[40,512]{1,0:T(8,128)(2,1)S(1)}, bf16[40,512]{1,0:T(8,128)(2,1)S(1)}) fusion(bf16[144,512]{1,0:T(8,128)(2,1)} %bitcast.72, bf16[144,512]{1,0:T(8,128)(2,1)S(1)} %bitcast.611), kind=kCustom, calls=%all-reduce-scatter.2 | all-reduce-scatter fusion | flops 163841 | bytes 377344
  340.1 3.8 collective-permute-start.8
  348.3 7.6 %reduce-scatter.21.cloned.1.call-done = bf16[128,512]{1,0:T(8,128)(2,1)} async-done(((bf16[512,512]{1,0:T(8,128)(2,1)}), bf16[128,512]{1,0:T(8,128)(2,1)}) %reduce-scatter.21.cloned.1.call-update) | async-done | bytes 131088
  357.7 23.0 %reduce-scatter.17.cloned.1.call-done = bf16[128,512]{1,0:T(8,128)(2,1)} async-done(((bf16[512,512]{1,0:T(8,128)(2,1)}), bf16[128,512]{1,0:T(8,128)(2,1)}) %reduce-scatter.17.cloned.1.call-update) | async-done | bytes 131088
  383.5 40.3 %all-reduce.12.cloned.1.call-done = (bf16[2,128,512]{1,2,0:T(8,128)(2,1)}, bf16[2,36,512]{2,1,0:T(8,128)(2,1)}, bf16[2,128,512]{1,2,0:T(8,128)(2,1)}) async-done(((bf16[2,128,512]{1,2,0:T(8,128)(2,1)}, bf16[2,36,512]{2,1,0:T(8,128)(2,1)}, bf16[2,128,512]{1,2,0:T(8,128)(2,1)}), (bf16[2,128,512]{1,2,0:T(8,128)(2,1)}, bf16[2,36,512]{2,1,0:T(8,128)(2,1)}, ...) | async-done | bytes 598032 | tf_op jit(solution)/shard_map/psum | solution.py:168
  (554 shorter events, 183.3 us)
Async XLA Ops:
  7.2 10.3 %copy-start.98 = (bf16[1,2,128,512]{3,2,1,0:T(8,128)(2,1)S(1)}, bf16[1,2,128,512]{3,2,1,0:T(8,128)(2,1)}, u32[]{:S(2)}) copy-start(bf16[1,2,128,512]{3,2,1,0:T(8,128)(2,1)} %param.13) | copy-start | bytes 786436
  7.2 339.0 %reduce-scatter.23.cloned.1.call-start = ((), (), s32[]{:S(2)}) async-start(), calls=%async_computation.7 | async-start | bytes 655360
  18.6 14.8 %copy-start = (bf16[256,512]{1,0:T(8,128)(2,1)}, bf16[256,512]{1,0:T(8,128)(2,1)S(1)}, u32[]{:S(2)}) copy-start(bf16[256,512]{1,0:T(8,128)(2,1)S(1)} %get-tuple-element.145) | copy-start | bytes 786436
  18.6 8.1 %copy-start.97 = (bf16[2,128,512]{2,1,0:T(8,128)(2,1)S(1)}, bf16[2,128,512]{2,1,0:T(8,128)(2,1)}, u32[]{:S(2)}) copy-start(bf16[2,128,512]{2,1,0:T(8,128)(2,1)} %param.17) | copy-start | bytes 786436
  18.6 8.8 %copy-start.93 = (bf16[2,36,512]{2,0,1:T(2,128)(2,1)S(1)}, bf16[2,36,512]{2,0,1:T(2,128)(2,1)}, u32[]{:S(2)}) copy-start(bf16[2,36,512]{2,0,1:T(2,128)(2,1)} %param.16) | copy-start | bytes 221188
  19.3 80.7 %collective-permute-start.1 = (bf16[1,1,128,512]{3,2,1,0:T(8,128)(2,1)}, bf16[1,1,128,512]{3,2,1,0:T(8,128)(2,1)}, u32[]{:S(2)}, u32[]{:S(2)}) collective-permute-start(bf16[1,1,128,512]{3,2,1,0:T(8,128)(2,1)} %get-tuple-element.136), channel_id=1, source_target_pairs={{4,0},{8,4},{12,8},{5,1},{9,5},{13,9},{6,2},{10,6},{14,10},{7,3},{... | collective-permute-start | bytes 393224 | tf_op jit(solution)/shard_map/ppermute | solution.py:21
  20.6 79.5 %collective-permute-start = (bf16[1,1,128,512]{3,2,1,0:T(8,128)(2,1)}, bf16[1,1,128,512]{3,2,1,0:T(8,128)(2,1)}, u32[]{:S(2)}, u32[]{:S(2)}) collective-permute-start(bf16[1,1,128,512]{3,2,1,0:T(8,128)(2,1)} %get-tuple-element.135), channel_id=1, source_target_pairs={{0,4},{4,8},{8,12},{1,5},{5,9},{9,13},{2,6},{6,10},{10,14},{3,7},{... | collective-permute-start | bytes 393224 | tf_op jit(solution)/shard_map/ppermute | solution.py:19
  88.6 11.5 %copy-start.1 = (bf16[256,512]{1,0:T(8,128)(2,1)S(1)}, bf16[256,512]{1,0:T(8,128)(2,1)}, u32[]{:S(2)}) copy-start(bf16[256,512]{1,0:T(8,128)(2,1)} %copy-done) | copy-start | bytes 786436
  107.8 3.6 copy-start.63
  113.9 7.1 %copy-start.62 = (bf16[1,2,128,512]{3,2,1,0:T(8,128)(2,1)S(1)}, bf16[1,2,128,512]{3,2,1,0:T(8,128)(2,1)}, u32[]{:S(2)}) copy-start(bf16[1,2,128,512]{3,2,1,0:T(8,128)(2,1)} %get-tuple-element.104) | copy-start | bytes 786436
  123.7 7.1 %copy-start.2 = (bf16[256,4,128]{0,2,1:T(8,128)(2,1)S(1)}, bf16[256,4,128]{0,2,1:T(8,128)(2,1)}, u32[]{:S(2)}) copy-start(bf16[256,4,128]{0,2,1:T(8,128)(2,1)} %copy.294) | copy-start | bytes 786436
  140.1 8.4 %copy-start.92 = (bf16[1,128,512]{2,1,0:T(8,128)(2,1)S(1)}, bf16[1,128,512]{2,1,0:T(8,128)(2,1)}, u32[]{:S(2)}) copy-start(bf16[1,128,512]{2,1,0:T(8,128)(2,1)} %get-tuple-element.140) | copy-start | bytes 393220
  141.9 33.2 %collective-permute-start.3 = (bf16[1,1,128,512]{3,2,1,0:T(8,128)(2,1)}, bf16[1,1,128,512]{3,2,1,0:T(8,128)(2,1)}, u32[]{:S(2)}, u32[]{:S(2)}) collective-permute-start(bf16[1,1,128,512]{3,2,1,0:T(8,128)(2,1)} %get-tuple-element.132), channel_id=1, source_target_pairs={{4,0},{8,4},{12,8},{5,1},{9,5},{13,9},{6,2},{10,6},{14,10},{7,3},{... | collective-permute-start | bytes 393224 | tf_op jit(solution)/shard_map/ppermute | solution.py:21
  143.2 32.0 %collective-permute-start.2 = (bf16[1,1,128,512]{3,2,1,0:T(8,128)(2,1)}, bf16[1,1,128,512]{3,2,1,0:T(8,128)(2,1)}, u32[]{:S(2)}, u32[]{:S(2)}) collective-permute-start(bf16[1,1,128,512]{3,2,1,0:T(8,128)(2,1)} %get-tuple-element.131), channel_id=1, source_target_pairs={{0,4},{4,8},{8,12},{1,5},{5,9},{9,13},{2,6},{6,10},{10,14},{3,7},{... | collective-permute-start | bytes 393224 | tf_op jit(solution)/shard_map/ppermute | solution.py:19
  173.7 10.5 %copy-start.48 = (bf16[4,128,128]{1,2,0:T(8,128)(2,1)}, bf16[4,128,128]{1,2,0:T(8,128)(2,1)S(1)}, u32[]{:S(2)}) copy-start(bf16[4,128,128]{1,2,0:T(8,128)(2,1)S(1)} %squeeze.117) | copy-start | bytes 393220
  179.0 2.2 copy-start.31
  179.3 2.1 copy-start.60
  186.1 2.8 copy-start.86
  186.1 2.8 copy-start.91
  188.8 8.2 %copy-start.119 = (f32[256,512]{1,0:T(8,128)}, f32[256,512]{1,0:T(8,128)S(1)}, u32[]{:S(2)}) copy-start(f32[256,512]{1,0:T(8,128)S(1)} %get-tuple-element.109) | copy-start | bytes 1572868
  220.8 7.8 %copy-start.76 = (bf16[4,128,128]{2,1,0:T(8,128)(2,1)S(1)}, bf16[4,128,128]{2,1,0:T(8,128)(2,1)}, u32[]{:S(2)}) copy-start(bf16[4,128,128]{2,1,0:T(8,128)(2,1)} %fusion.61) | copy-start | bytes 393220
  221.3 35.3 %collective-permute-start.5 = (bf16[1,1,128,512]{3,2,1,0:T(8,128)(2,1)S(1)}, bf16[1,1,128,512]{3,2,1,0:T(8,128)(2,1)}, u32[]{:S(2)}, u32[]{:S(2)}) collective-permute-start(bf16[1,1,128,512]{3,2,1,0:T(8,128)(2,1)S(1)} %copy.402), channel_id=1, source_target_pairs={{4,0},{8,4},{12,8},{5,1},{9,5},{13,9},{6,2},{10,6},{14,10},{7,3},{... | collective-permute-start | bytes 393224 | tf_op jit(solution)/shard_map/ppermute | solution.py:21
  223.4 33.2 %collective-permute-start.4 = (bf16[1,1,128,512]{3,2,1,0:T(8,128)(2,1)}, bf16[1,1,128,512]{3,2,1,0:T(8,128)(2,1)}, u32[]{:S(2)}, u32[]{:S(2)}) collective-permute-start(bf16[1,1,128,512]{3,2,1,0:T(8,128)(2,1)} %copy.401), channel_id=1, source_target_pairs={{0,4},{4,8},{8,12},{1,5},{5,9},{9,13},{2,6},{6,10},{10,14},{3,7},{... | collective-permute-start | bytes 393224 | tf_op jit(solution)/shard_map/ppermute | solution.py:19
  248.6 2.4 copy-start.107
  248.6 3.0 copy-start.109
  248.6 3.6 copy-start.110
  248.6 4.2 copy-start.112
  248.6 4.8 %copy-start.114 = (bf16[1,16,512]{2,1,0:T(8,128)(2,1)S(1)}, bf16[1,16,512]{2,1,0:T(8,128)(2,1)}, u32[]{:S(2)}) copy-start(bf16[1,16,512]{2,1,0:T(8,128)(2,1)} %stack_reshape.88) | copy-start | bytes 49156
  249.6 97.7 %reduce-scatter.19.cloned.1.call-start = ((), (), s32[]{:S(2)}) async-start(), calls=%async_computation.5 | async-start | bytes 655360
  256.6 2.1 copy-start.90
  287.0 9.7 %copy-start.78 = (bf16[4,128,128]{2,1,0:T(8,128)(2,1)S(1)}, bf16[4,128,128]{2,1,0:T(8,128)(2,1)}, u32[]{:S(2)}) copy-start(bf16[4,128,128]{2,1,0:T(8,128)(2,1)} %fusion.79) | copy-start | bytes 393220
  289.2 37.2 %collective-permute-start.7 = (bf16[1,1,128,512]{3,2,1,0:T(8,128)(2,1)}, bf16[1,1,128,512]{3,2,1,0:T(8,128)(2,1)}, u32[]{:S(2)}, u32[]{:S(2)}) collective-permute-start(bf16[1,1,128,512]{3,2,1,0:T(8,128)(2,1)} %copy.406), channel_id=1, source_target_pairs={{4,0},{8,4},{12,8},{5,1},{9,5},{13,9},{6,2},{10,6},{14,10},{7,3},{... | collective-permute-start | bytes 393224 | tf_op jit(solution)/shard_map/ppermute | solution.py:21
  291.3 35.1 %collective-permute-start.6 = (bf16[1,1,128,512]{3,2,1,0:T(8,128)(2,1)}, bf16[1,1,128,512]{3,2,1,0:T(8,128)(2,1)}, u32[]{:S(2)}, u32[]{:S(2)}) collective-permute-start(bf16[1,1,128,512]{3,2,1,0:T(8,128)(2,1)} %copy.405), channel_id=1, source_target_pairs={{0,4},{4,8},{8,12},{1,5},{5,9},{9,13},{2,6},{6,10},{10,14},{3,7},{... | collective-permute-start | bytes 393224 | tf_op jit(solution)/shard_map/ppermute | solution.py:19
  304.8 2.1 copy-start.13
  305.4 2.4 copy-start.95
  307.8 2.4 copy-start.113
  307.8 2.4 copy-start.115
  307.8 2.4 copy-start.7
  310.1 45.8 %reduce-scatter.21.cloned.1.call-start = ((), (), s32[]{:S(2)}) async-start(), calls=%async_computation.6 | async-start | bytes 655360
  325.7 2.7 copy-start.87
  325.7 55.0 %reduce-scatter.17.cloned.1.call-start = ((), (), s32[]{:S(2)}) async-start(), calls=%async_computation.4 | async-start | bytes 655360
  329.0 14.9 %copy-start.117 = (u32[32]{0:T(128)S(1)}, u32[32]{0:T(128)}, u32[]{:S(2)}) copy-start(u32[32]{0:T(128)} %constant.395) | copy-start | bytes 388
  330.0 93.8 %all-reduce.12.cloned.1.call-start = ((), (), s32[]{:S(2)}) async-start(), calls=%async_computation.8 | async-start | bytes 1212416 | tf_op jit(solution)/shard_map/psum | solution.py:168
  338.8 6.3 %collective-permute-start.9 = (bf16[12,512]{1,0:T(8,128)(2,1)S(1)}, bf16[12,512]{1,0:T(8,128)(2,1)S(1)}, u32[]{:S(2)}, u32[]{:S(2)}) collective-permute-start(bf16[12,512]{1,0:T(8,128)(2,1)S(1)} %slice.573), channel_id=1, source_target_pairs={{0,1},{1,2},{2,3},{4,5},{5,6},{6,7},{8,9},{9,10},{10,11},{12,13},{... | collective-permute-start | bytes 36872
  340.1 5.2 %collective-permute-start.8 = (bf16[12,512]{1,0:T(8,128)(2,1)S(1)}, bf16[12,512]{1,0:T(8,128)(2,1)S(1)}, u32[]{:S(2)}, u32[]{:S(2)}) collective-permute-start(bf16[12,512]{1,0:T(8,128)(2,1)S(1)} %slice.572), channel_id=1, source_target_pairs={{0,1},{1,2},{2,3},{4,5},{5,6},{6,7},{8,9},{9,10},{10,11},{12,13},{... | collective-permute-start | bytes 36872
  348.3 34.2 %copy-start.20 = (bf16[1,512,512]{2,1,0:T(8,128)(2,1)S(1)}, bf16[1,512,512]{2,1,0:T(8,128)(2,1)}, u32[]{:S(2)}) copy-start(bf16[1,512,512]{2,1,0:T(8,128)(2,1)} %copy-done.19) | copy-start | bytes 1572868
  348.3 34.2 %copy-start.66 = (f32[256,512]{1,0:T(8,128)S(1)}, f32[256,512]{1,0:T(8,128)}, u32[]{:S(2)}) copy-start(f32[256,512]{1,0:T(8,128)} %copy-done.64) | copy-start | bytes 1572868
  423.8 2.8 copy-start.96
  (90 other events, 115.9 us)
Sparse Core Ops, SparseCore 0:
  249.7 21.4 reduce-scatter.22
  310.2 21.4 reduce-scatter.18
  334.2 21.6 reduce-scatter.20
  359.0 21.6 reduce-scatter.16
  383.7 40.0 all-reduce.11
where the time goes:
time: 442 us; the launch traced here: 435 us
  local copies, waits for them, and re-layouts  196 us (44%)
  waiting for transfers between devices  71 us (16%)
  blocking collectives  54.3 us (12%)
  matrix products  44.2 us (10%)
  starting transfers between devices  31.6 us (7%)
  other arithmetic  20.9 us (5%)
  between operations  17.1 us (4%)
    reshape x52, local copies, waits for them, and re-layouts, grouped_taps(): window = window.reshape(-1, kernel.shape[1], kernel.shape[2])  52.9 us
    squeeze x18, local copies, waits for them, and re-layouts, grouped_taps(): kernel[tap_index]  42.2 us
    psum x1, waiting for transfers between devices, body(): lax.psum(jnp.stack([entry[0] for entry in shares]).astype(jnp.bfloat16),...  40.3 us
    unnamed x283, local copies, waits for them, and re-layouts  31.7 us
    unnamed x11, waiting for transfers between devices  30.7 us
    ppermute x4, starting transfers between devices, extended_2(): lax.ppermute(tail, axis, [(i, (i + 1) % count) for i in range(ends)])  21 us
    all_gather x2, blocking collectives, body(): lax.all_gather(weight_in[block_index], 'shard', axis=0, tiled=True)  17.6 us
    dot_general x36, matrix products, grouped_taps(): jnp.einsum(pattern, window, kernel[tap_index], preferred_element_type=jnp...  16.2 us
  transfers between devices with their start and end apart: 15, of which 3 were waited for; matrix products, arithmetic and copies ran while one was open for 38% of the time, Pallas kernels for 0%

commit v1 on v0

--- a/solution.py
+++ b/solution.py
@@ -128,8 +128,9 @@
                 "psi,pso->sio", window, slope_sections, preferred_element_type=jnp.float32
             )
             blockwise = blockwise.reshape(sections, members, group_width, members, group_width)
-            diagonal_part = jnp.diagonal(blockwise, axis1=1, axis2=3)
-            tap_terms.append(diagonal_part.transpose(1, 0, 3, 2).reshape(group_width, hidden_width))
+            same = jnp.eye(members, dtype=jnp.float32)[None, :, None, :, None]
+            diagonal_part = jnp.sum(blockwise * same, axis=1)
+            tap_terms.append(diagonal_part.transpose(1, 0, 2, 3).reshape(group_width, hidden_width))
         part_group = jnp.stack(tap_terms).reshape(9 * group_width, hidden_width)
         slope_grid = slope_two.reshape(tile_count, height, across, hidden_width)
         padded_slope = jnp.pad(slope_grid, ((0, 0), (2, 2), (1, 1), (0, 0)))

time: 442 us -> 482 us (1.090)
  other arithmetic: 20.9 us -> 36.9 us
  local copies, waits for them, and re-layouts: 196 us -> 206 us
  waiting for transfers between devices: 71 us -> 77.2 us
  matrix products: 44.2 us -> 49.6 us
    reshape x36 -> x18, local copies, waits for them, and re-layouts: 15.9 us -> 37.3 us  [body(): blockwise.reshape(sections, members, group_width, members, group_width)]
    reduce_sum x0 -> x1, other arithmetic: none -> 15.7 us  [body(): diagonal_part = jnp.sum(blockwise * same, axis=1)]
    gather x18 -> x0, local copies, waits for them, and re-layouts: 10.7 us -> none  [body(): diagonal_part = jnp.diagonal(blockwise, axis1=1, axis2=3)]
    another operation x20, local copies, waits for them, and re-layouts: 12.3 us -> 3.87 us  [body(): part_group = jnp.stack(tap_terms).reshape(9 * group_width, hidden_width)]
    reshape x52, local copies, waits for them, and re-layouts: 52.9 us -> 60.5 us  [grouped_taps(): window = window.reshape(-1, kernel.shape[1], kernel.shape[2])]
    unnamed x283 -> x273, local copies, waits for them, and re-layouts: 31.7 us -> 24.9 us
    unnamed x11, waiting for transfers between devices: 30.7 us -> 36.8 us
    transpose x18, local copies, waits for them, and re-layouts: 1.63 us -> 7.01 us  [body(): diagonal_part.transpose(1, 0, 2, 3).reshape(group_width, hidden_width)]
  transfers between devices with their start and end apart: 15 -> 15, of which waited for: 3 -> 3; matrix products, arithmetic and copies ran while one was open for 38% -> 42% of each run, Pallas kernels for 0% -> 0%
where the time goes in v1:
time: 482 us; the launch traced here: 473 us
  local copies, waits for them, and re-layouts  206 us (43%)
  waiting for transfers between devices  77.2 us (16%)
  blocking collectives  55.2 us (11%)
  matrix products  49.6 us (10%)
  other arithmetic  36.9 us (8%)
  starting transfers between devices  32.2 us (7%)
  between operations  16.6 us (3%)
    reshape x52, local copies, waits for them, and re-layouts, grouped_taps(): window = window.reshape(-1, kernel.shape[1], kernel.shape[2])  60.5 us
    squeeze x18, local copies, waits for them, and re-layouts, grouped_taps(): kernel[tap_index]  41.4 us
    psum x1, waiting for transfers between devices, body(): lax.psum(jnp.stack([entry[0] for entry in shares]).astype(jnp.bfloat16),...  40.3 us
    reshape x18, local copies, waits for them, and re-layouts, body(): blockwise.reshape(sections, members, group_width, members, group_width)  37.3 us
    unnamed x11, waiting for transfers between devices  36.8 us
    unnamed x273, local copies, waits for them, and re-layouts  24.9 us
    ppermute x4, starting transfers between devices, extended_2(): lax.ppermute(tail, axis, [(i, (i + 1) % count) for i in range(ends)])  20.9 us
    dot_general x36, matrix products, grouped_taps(): jnp.einsum(pattern, window, kernel[tap_index], preferred_element_type=jnp...  18.3 us
  transfers between devices with their start and end apart: 15, of which 3 were waited for; matrix products, arithmetic and copies ran while one was open for 42% of the time, Pallas kernels for 0%

profile of v1, /device:TPU:0, one launch (start us, length us, event | category | flops | bytes accessed | tf_op | source)
XLA Modules:
  0.0 473.4 jit_solution(3516267203745144367)
XLA Ops:
  8.9 8.6 %all-gather.1 = bf16[1,512,512]{2,1,0:T(8,128)(2,1)S(1)} all-gather(bf16[1,128,512]{2,1,0:T(8,128)(2,1)S(1)} %get-tuple-element.160), channel_id=3, replica_groups=mesh['groups'=2,'rows'=4,'shard'=4] {'shard'}, dimensions={1}, use_global_device_ids=true | all-gather | bytes 655360 | tf_op jit(solution)/shard_map/all_gather | solution.py:70
  18.3 2.1 multiply_convert_fusion.5
  22.4 5.2 %collective-permute-start = (bf16[1,1,128,512]{3,2,1,0:T(8,128)(2,1)}, bf16[1,1,128,512]{3,2,1,0:T(8,128)(2,1)}, u32[]{:S(2)}, u32[]{:S(2)}) collective-permute-start(bf16[1,1,128,512]{3,2,1,0:T(8,128)(2,1)} %get-tuple-element.158), channel_id=1, source_target_pairs={{0,4},{4,8},{8,12},{1,5},{5,9},{9,13},{2,6},{6,10},{10,14},{3,7},{... | collective-permute-start | bytes 393224 | tf_op jit(solution)/shard_map/ppermute | solution.py:19
  29.4 5.9 %all-gather = bf16[1,144,512]{2,0,1:T(2,128)(2,1)S(1)} all-gather(bf16[1,36,512]{2,0,1:T(2,128)(2,1)S(1)} %get-tuple-element.164), channel_id=2, replica_groups=mesh['groups'=2,'rows'=4,'shard'=4] {'shard'}, dimensions={1}, use_global_device_ids=true | all-gather | bytes 184320 | tf_op jit(solution)/shard_map/all_gather | solution.py:71
  38.4 6.0 %all-gather.3 = bf16[1,144,512]{2,0,1:T(2,128)(2,1)S(1)} all-gather(bf16[1,36,512]{2,0,1:T(2,128)(2,1)S(1)} %get-tuple-element.165), channel_id=5, replica_groups=mesh['groups'=2,'rows'=4,'shard'=4] {'shard'}, dimensions={1}, use_global_device_ids=true | all-gather | bytes 184320 | tf_op jit(solution)/shard_map/all_gather | solution.py:71
  47.7 9.4 %all-gather.4 = bf16[1,512,512]{2,1,0:T(8,128)(2,1)} all-gather(bf16[1,128,512]{2,1,0:T(8,128)(2,1)} %get-tuple-element.161), channel_id=6, replica_groups=mesh['groups'=2,'rows'=4,'shard'=4] {'shard'}, dimensions={1}, use_global_device_ids=true | all-gather | bytes 655360 | tf_op jit(solution)/shard_map/all_gather | solution.py:70
  57.0 4.3 broadcast_multiply_fusion.1
  61.4 8.6 %fusion.110 = (bf16[1,4,8,16,8,16]{3,2,5,4,1,0:T(8,128)(2,1)S(1)}, bf16[1,4,8,16,8,16]{3,2,5,4,1,0:T(8,128)(2,1)S(1)}, bf16[1,4,8,16,8,16]{3,2,5,4,1,0:T(8,128)(...) fusion(bf16[9,4,8,16,8,16]{3,2,5,4,1,0:T(8,128)(2,1)} %get-tupl, ...), kind=kLoop, calls=%fused_computation.267 | loop fusion | bytes 4718592 | tf_op jit(solution)/shard_map/slice | solution.py:55
  70.0 2.0 squeeze.97
  72.0 2.6 squeeze.99
  74.6 2.6 squeeze.100
  77.2 2.6 squeeze.101
  79.8 2.6 squeeze.102
  82.4 2.6 squeeze.103
  85.0 2.6 squeeze.104
  87.7 2.6 squeeze.105
  90.3 2.6 squeeze.106
  92.9 8.8 %all-gather.2 = bf16[1,512,512]{2,1,0:T(8,128)(2,1)} all-gather(bf16[1,128,512]{2,1,0:T(8,128)(2,1)} %get-tuple-element.162), channel_id=4, replica_groups=mesh['groups'=2,'rows'=4,'shard'=4] {'shard'}, dimensions={1}, use_global_device_ids=true | all-gather | bytes 655360 | tf_op jit(solution)/shard_map/all_gather | solution.py:72
  137.8 2.1 copy.447
  144.7 5.2 %collective-permute-start.2 = (bf16[1,1,128,512]{3,2,1,0:T(8,128)(2,1)}, bf16[1,1,128,512]{3,2,1,0:T(8,128)(2,1)}, u32[]{:S(2)}, u32[]{:S(2)}) collective-permute-start(bf16[1,1,128,512]{3,2,1,0:T(8,128)(2,1)} %get-tuple-element.154), channel_id=1, source_target_pairs={{0,4},{4,8},{8,12},{1,5},{5,9},{9,13},{2,6},{6,10},{10,14},{3,7},{... | collective-permute-start | bytes 393224 | tf_op jit(solution)/shard_map/ppermute | solution.py:19
  149.9 7.2 %all-gather.5 = bf16[1,512,512]{2,1,0:T(8,128)(2,1)} all-gather(bf16[1,128,512]{2,1,0:T(8,128)(2,1)S(1)} %copy-done.94), channel_id=7, replica_groups=mesh['groups'=2,'rows'=4,'shard'=4] {'shard'}, dimensions={1}, use_global_device_ids=true | all-gather | bytes 655360 | tf_op jit(solution)/shard_map/all_gather | solution.py:72
  157.1 2.6 squeeze.109
  159.7 2.6 squeeze.111
  162.3 2.6 squeeze.112
  164.9 2.6 squeeze.113
  167.5 2.6 squeeze.114
  170.1 2.8 squeeze.115
  185.2 2.7 convert_multiply_fusion
  206.9 2.0 reshape.661
  208.9 2.0 reshape.662
  222.8 5.2 %collective-permute-start.4 = (bf16[1,1,128,512]{3,2,1,0:T(8,128)(2,1)}, bf16[1,1,128,512]{3,2,1,0:T(8,128)(2,1)}, u32[]{:S(2)}, u32[]{:S(2)}) collective-permute-start(bf16[1,1,128,512]{3,2,1,0:T(8,128)(2,1)} %copy.459), channel_id=1, source_target_pairs={{0,4},{4,8},{8,12},{1,5},{5,9},{9,13},{2,6},{6,10},{10,14},{3,7},{... | collective-permute-start | bytes 393224 | tf_op jit(solution)/shard_map/ppermute | solution.py:19
  236.9 2.0 reshape.696
  240.8 2.0 reshape.698
  260.7 2.3 pad_slice_fusion
  273.1 2.0 reshape.674
  279.0 2.0 reshape.677
  294.0 5.3 %collective-permute-start.6 = (bf16[1,1,128,512]{3,2,1,0:T(8,128)(2,1)}, bf16[1,1,128,512]{3,2,1,0:T(8,128)(2,1)}, u32[]{:S(2)}, u32[]{:S(2)}) collective-permute-start(bf16[1,1,128,512]{3,2,1,0:T(8,128)(2,1)} %copy.463), channel_id=1, source_target_pairs={{0,4},{4,8},{8,12},{1,5},{5,9},{9,13},{2,6},{6,10},{10,14},{3,7},{... | collective-permute-start | bytes 393224 | tf_op jit(solution)/shard_map/ppermute | solution.py:19
  301.3 2.9 reshape.683
  306.1 2.9 reshape.685
  311.0 3.0 reshape.687
  315.8 2.9 reshape.689
  320.6 15.7 %multiply_reduce_fusion.9 = (bf16[4,16,8,16]{3,2,1,0:T(8,128)(2,1)}, bf16[4,16,8,16]{3,2,1,0:T(8,128)(2,1)}, bf16[4,16,8,16]{3,2,1,0:T(8,128)(2,1)S(1)}, bf16[4,...) fusion(f32[4,8,16,8,16]{4,3,2,1,0:T(8,128)} %reshape.690, ...), kind=kLoop, calls=%fused_computation.29 | loop fusion | flops 2211840 | bytes 5013760 | tf_op jit(solution)/shard_map/reduce_sum | solution.py:132
  343.6 2.3 convolution_convert_fusion.2
  360.8 9.3 %fusion.109 = (bf16[40,512]{1,0:T(8,128)(2,1)S(1)}, bf16[40,512]{1,0:T(8,128)(2,1)S(1)}) fusion(bf16[144,512]{1,0:T(8,128)(2,1)S(1)} %bitcast.538, bf16[144,512]{1,0:T(8,128)(2,1)} %bitcast.42), kind=kCustom, calls=%all-reduce-scatter.2 | all-reduce-scatter fusion | flops 163841 | bytes 377344
  371.6 4.3 collective-permute-start.8
  380.3 13.7 %reduce-scatter.21.cloned.1.call-done = bf16[128,512]{1,0:T(8,128)(2,1)} async-done(((bf16[512,512]{1,0:T(8,128)(2,1)}), bf16[128,512]{1,0:T(8,128)(2,1)}) %reduce-scatter.21.cloned.1.call-update) | async-done | bytes 131088
  395.8 23.0 %reduce-scatter.17.cloned.1.call-done = bf16[128,512]{1,0:T(8,128)(2,1)} async-done(((bf16[512,512]{1,0:T(8,128)(2,1)}), bf16[128,512]{1,0:T(8,128)(2,1)}) %reduce-scatter.17.cloned.1.call-update) | async-done | bytes 131088
  421.6 40.3 %all-reduce.12.cloned.1.call-done = (bf16[2,128,512]{1,2,0:T(8,128)(2,1)}, bf16[2,36,512]{2,1,0:T(8,128)(2,1)}, bf16[2,128,512]{1,2,0:T(8,128)(2,1)}) async-done(((bf16[2,128,512]{1,2,0:T(8,128)(2,1)}, bf16[2,36,512]{2,1,0:T(8,128)(2,1)}, bf16[2,128,512]{1,2,0:T(8,128)(2,1)}), (bf16[2,128,512]{1,2,0:T(8,128)(2,1)}, bf16[2,36,512]{2,1,0:T(8,128)(2,1)}, ...) | async-done | bytes 598032 | tf_op jit(solution)/shard_map/psum | solution.py:169
  (510 shorter events, 197.0 us)
Async XLA Ops:
  7.2 371.0 %reduce-scatter.23.cloned.1.call-start = ((), (), s32[]{:S(2)}) async-start(), calls=%async_computation.7 | async-start | bytes 655360
  17.5 11.0 %copy-start.108 = (bf16[2,128,512]{2,1,0:T(8,128)(2,1)S(1)}, bf16[2,128,512]{2,1,0:T(8,128)(2,1)}, u32[]{:S(2)}) copy-start(bf16[2,128,512]{2,1,0:T(8,128)(2,1)} %param.17) | copy-start | bytes 786436
  18.3 11.0 %copy-start.104 = (bf16[2,36,512]{2,0,1:T(2,128)(2,1)S(1)}, bf16[2,36,512]{2,0,1:T(2,128)(2,1)}, u32[]{:S(2)}) copy-start(bf16[2,36,512]{2,0,1:T(2,128)(2,1)} %param.16) | copy-start | bytes 221188
  20.4 16.7 %copy-start = (bf16[256,512]{1,0:T(8,128)(2,1)}, bf16[256,512]{1,0:T(8,128)(2,1)S(1)}, u32[]{:S(2)}) copy-start(bf16[256,512]{1,0:T(8,128)(2,1)S(1)} %get-tuple-element.168) | copy-start | bytes 786436
  21.1 80.6 %collective-permute-start.1 = (bf16[1,1,128,512]{3,2,1,0:T(8,128)(2,1)}, bf16[1,1,128,512]{3,2,1,0:T(8,128)(2,1)}, u32[]{:S(2)}, u32[]{:S(2)}) collective-permute-start(bf16[1,1,128,512]{3,2,1,0:T(8,128)(2,1)} %get-tuple-element.159), channel_id=1, source_target_pairs={{4,0},{8,4},{12,8},{5,1},{9,5},{13,9},{6,2},{10,6},{14,10},{7,3},{... | collective-permute-start | bytes 393224 | tf_op jit(solution)/shard_map/ppermute | solution.py:21
  22.4 79.3 %collective-permute-start = (bf16[1,1,128,512]{3,2,1,0:T(8,128)(2,1)}, bf16[1,1,128,512]{3,2,1,0:T(8,128)(2,1)}, u32[]{:S(2)}, u32[]{:S(2)}) collective-permute-start(bf16[1,1,128,512]{3,2,1,0:T(8,128)(2,1)} %get-tuple-element.158), channel_id=1, source_target_pairs={{0,4},{4,8},{8,12},{1,5},{5,9},{9,13},{2,6},{6,10},{10,14},{3,7},{... | collective-permute-start | bytes 393224 | tf_op jit(solution)/shard_map/ppermute | solution.py:19
  85.0 16.7 %copy-start.1 = (bf16[256,512]{1,0:T(8,128)(2,1)S(1)}, bf16[256,512]{1,0:T(8,128)(2,1)}, u32[]{:S(2)}) copy-start(bf16[256,512]{1,0:T(8,128)(2,1)} %copy-done) | copy-start | bytes 786436
  109.3 7.1 %copy-start.80 = (bf16[1,2,128,512]{3,2,1,0:T(8,128)(2,1)S(1)}, bf16[1,2,128,512]{3,2,1,0:T(8,128)(2,1)}, u32[]{:S(2)}) copy-start(bf16[1,2,128,512]{3,2,1,0:T(8,128)(2,1)} %get-tuple-element.129) | copy-start | bytes 786436
  119.0 14.2 %copy-start.2 = (bf16[256,4,128]{0,2,1:T(8,128)(2,1)S(1)}, bf16[256,4,128]{0,2,1:T(8,128)(2,1)}, u32[]{:S(2)}) copy-start(bf16[256,4,128]{0,2,1:T(8,128)(2,1)} %copy.370) | copy-start | bytes 786436
  141.5 8.3 %copy-start.94 = (bf16[1,128,512]{2,1,0:T(8,128)(2,1)S(1)}, bf16[1,128,512]{2,1,0:T(8,128)(2,1)}, u32[]{:S(2)}) copy-start(bf16[1,128,512]{2,1,0:T(8,128)(2,1)} %get-tuple-element.163) | copy-start | bytes 393220
  143.4 32.4 %collective-permute-start.3 = (bf16[1,1,128,512]{3,2,1,0:T(8,128)(2,1)}, bf16[1,1,128,512]{3,2,1,0:T(8,128)(2,1)}, u32[]{:S(2)}, u32[]{:S(2)}) collective-permute-start(bf16[1,1,128,512]{3,2,1,0:T(8,128)(2,1)} %get-tuple-element.155), channel_id=1, source_target_pairs={{4,0},{8,4},{12,8},{5,1},{9,5},{13,9},{6,2},{10,6},{14,10},{7,3},{... | collective-permute-start | bytes 393224 | tf_op jit(solution)/shard_map/ppermute | solution.py:21
  144.7 31.1 %collective-permute-start.2 = (bf16[1,1,128,512]{3,2,1,0:T(8,128)(2,1)}, bf16[1,1,128,512]{3,2,1,0:T(8,128)(2,1)}, u32[]{:S(2)}, u32[]{:S(2)}) collective-permute-start(bf16[1,1,128,512]{3,2,1,0:T(8,128)(2,1)} %get-tuple-element.154), channel_id=1, source_target_pairs={{0,4},{4,8},{8,12},{1,5},{5,9},{9,13},{2,6},{6,10},{10,14},{3,7},{... | collective-permute-start | bytes 393224 | tf_op jit(solution)/shard_map/ppermute | solution.py:19
  174.9 8.8 %copy-start.52 = (bf16[4,128,128]{1,2,0:T(8,128)(2,1)}, bf16[4,128,128]{1,2,0:T(8,128)(2,1)S(1)}, u32[]{:S(2)}) copy-start(bf16[4,128,128]{1,2,0:T(8,128)(2,1)S(1)} %squeeze.117) | copy-start | bytes 393220
  175.6 8.3 %copy-start.50 = (bf16[4,128,128]{1,2,0:T(8,128)(2,1)}, bf16[4,128,128]{1,2,0:T(8,128)(2,1)S(1)}, u32[]{:S(2)}) copy-start(bf16[4,128,128]{1,2,0:T(8,128)(2,1)S(1)} %squeeze.118) | copy-start | bytes 393220
  187.9 7.8 %copy-start.114 = (f32[256,512]{1,0:T(8,128)}, f32[256,512]{1,0:T(8,128)S(1)}, u32[]{:S(2)}) copy-start(f32[256,512]{1,0:T(8,128)S(1)} %get-tuple-element.132) | copy-start | bytes 1572868
  220.7 27.2 %collective-permute-start.5 = (bf16[1,1,128,512]{3,2,1,0:T(8,128)(2,1)}, bf16[1,1,128,512]{3,2,1,0:T(8,128)(2,1)}, u32[]{:S(2)}, u32[]{:S(2)}) collective-permute-start(bf16[1,1,128,512]{3,2,1,0:T(8,128)(2,1)} %copy.460), channel_id=1, source_target_pairs={{4,0},{8,4},{12,8},{5,1},{9,5},{13,9},{6,2},{10,6},{14,10},{7,3},{... | collective-permute-start | bytes 393224 | tf_op jit(solution)/shard_map/ppermute | solution.py:21
  222.0 8.5 %copy-start.66 = (f32[4,128,128]{2,1,0:T(8,128)S(1)}, f32[4,128,128]{2,1,0:T(8,128)}, u32[]{:S(2)}) copy-start(f32[4,128,128]{2,1,0:T(8,128)} %fusion.61) | copy-start | bytes 786436
  222.8 25.1 %collective-permute-start.4 = (bf16[1,1,128,512]{3,2,1,0:T(8,128)(2,1)}, bf16[1,1,128,512]{3,2,1,0:T(8,128)(2,1)}, u32[]{:S(2)}, u32[]{:S(2)}) collective-permute-start(bf16[1,1,128,512]{3,2,1,0:T(8,128)(2,1)} %copy.459), channel_id=1, source_target_pairs={{0,4},{4,8},{8,12},{1,5},{5,9},{9,13},{2,6},{6,10},{10,14},{3,7},{... | collective-permute-start | bytes 393224 | tf_op jit(solution)/shard_map/ppermute | solution.py:19
  246.7 132.6 %reduce-scatter.19.cloned.1.call-start = ((), (), s32[]{:S(2)}) async-start(), calls=%async_computation.5 | async-start | bytes 655360
  252.5 4.6 copy-start.12
  253.4 4.6 copy-start.14
  254.3 4.6 copy-start.16
  255.2 4.6 copy-start.3
  273.1 7.9 %copy-start.49 = (bf16[4,128,128]{1,2,0:T(8,128)(2,1)S(1)}, bf16[4,128,128]{1,2,0:T(8,128)(2,1)}, u32[]{:S(2)}) copy-start(bf16[4,128,128]{1,2,0:T(8,128)(2,1)} %squeeze.99) | copy-start | bytes 393220
  287.1 12.2 %copy-start.74 = (f32[4,128,128]{2,1,0:T(8,128)S(1)}, f32[4,128,128]{2,1,0:T(8,128)}, u32[]{:S(2)}) copy-start(f32[4,128,128]{2,1,0:T(8,128)} %fusion.63) | copy-start | bytes 786436
  291.0 63.8 %collective-permute-start.7 = (bf16[1,1,128,512]{3,2,1,0:T(8,128)(2,1)S(1)}, bf16[1,1,128,512]{3,2,1,0:T(8,128)(2,1)}, u32[]{:S(2)}, u32[]{:S(2)}) collective-permute-start(bf16[1,1,128,512]{3,2,1,0:T(8,128)(2,1)S(1)} %copy.464), channel_id=1, source_target_pairs={{4,0},{8,4},{12,8},{5,1},{9,5},{13,9},{6,2},{10,6},{14,10},{7,3},{... | collective-permute-start | bytes 393224 | tf_op jit(solution)/shard_map/ppermute | solution.py:21
  294.0 60.8 %collective-permute-start.6 = (bf16[1,1,128,512]{3,2,1,0:T(8,128)(2,1)}, bf16[1,1,128,512]{3,2,1,0:T(8,128)(2,1)}, u32[]{:S(2)}, u32[]{:S(2)}) collective-permute-start(bf16[1,1,128,512]{3,2,1,0:T(8,128)(2,1)} %copy.463), channel_id=1, source_target_pairs={{0,4},{4,8},{8,12},{1,5},{5,9},{9,13},{2,6},{6,10},{10,14},{3,7},{... | collective-permute-start | bytes 393224 | tf_op jit(solution)/shard_map/ppermute | solution.py:19
  336.3 4.9 %copy-start.103 = (bf16[4,16,8,16]{3,2,1,0:T(8,128)(2,1)S(1)}, bf16[4,16,8,16]{3,2,1,0:T(8,128)(2,1)}, u32[]{:S(2)}) copy-start(bf16[4,16,8,16]{3,2,1,0:T(8,128)(2,1)} %get-tuple-element.86) | copy-start | bytes 49156
  336.3 5.1 %copy-start.102 = (bf16[4,16,8,16]{3,2,1,0:T(8,128)(2,1)S(1)}, bf16[4,16,8,16]{3,2,1,0:T(8,128)(2,1)}, u32[]{:S(2)}) copy-start(bf16[4,16,8,16]{3,2,1,0:T(8,128)(2,1)} %get-tuple-element.87) | copy-start | bytes 49156
  336.3 5.3 %copy-start.101 = (bf16[4,16,8,16]{3,2,1,0:T(8,128)(2,1)S(1)}, bf16[4,16,8,16]{3,2,1,0:T(8,128)(2,1)}, u32[]{:S(2)}) copy-start(bf16[4,16,8,16]{3,2,1,0:T(8,128)(2,1)} %get-tuple-element.88) | copy-start | bytes 49156
  336.3 5.5 %copy-start.100 = (bf16[4,16,8,16]{3,2,1,0:T(8,128)(2,1)S(1)}, bf16[4,16,8,16]{3,2,1,0:T(8,128)(2,1)}, u32[]{:S(2)}) copy-start(bf16[4,16,8,16]{3,2,1,0:T(8,128)(2,1)} %get-tuple-element.89) | copy-start | bytes 49156
  336.3 5.8 %copy-start.99 = (bf16[4,16,8,16]{3,2,1,0:T(8,128)(2,1)S(1)}, bf16[4,16,8,16]{3,2,1,0:T(8,128)(2,1)}, u32[]{:S(2)}) copy-start(bf16[4,16,8,16]{3,2,1,0:T(8,128)(2,1)} %get-tuple-element.90) | copy-start | bytes 49156
  336.3 6.0 %copy-start.98 = (bf16[4,16,8,16]{3,2,1,0:T(8,128)(2,1)S(1)}, bf16[4,16,8,16]{3,2,1,0:T(8,128)(2,1)}, u32[]{:S(2)}) copy-start(bf16[4,16,8,16]{3,2,1,0:T(8,128)(2,1)} %get-tuple-element.74) | copy-start | bytes 49156
  337.7 5.0 %copy-start.97 = (bf16[4,16,8,16]{3,2,1,0:T(8,128)(2,1)S(1)}, bf16[4,16,8,16]{3,2,1,0:T(8,128)(2,1)}, u32[]{:S(2)}) copy-start(bf16[4,16,8,16]{3,2,1,0:T(8,128)(2,1)} %get-tuple-element.76) | copy-start | bytes 49156
  338.9 4.7 copy-start.106
  342.7 4.8 %copy-start.93 = (bf16[1,1,128,512]{3,2,1,0:T(8,128)(2,1)S(1)}, bf16[1,1,128,512]{3,2,1,0:T(8,128)(2,1)}, u32[]{:S(2)}) copy-start(bf16[1,1,128,512]{3,2,1,0:T(8,128)(2,1)} %copy.463) | copy-start | bytes 393220
  343.6 4.0 copy-start.90
  345.9 48.1 %reduce-scatter.21.cloned.1.call-start = ((), (), s32[]{:S(2)}) async-start(), calls=%async_computation.6 | async-start | bytes 655360
  349.3 4.3 copy-start.96
  349.6 4.3 copy-start.95
  351.4 5.4 %copy-start.88 = (f32[256,512]{1,0:T(8,128)S(1)}, f32[256,512]{1,0:T(8,128)}, u32[]{:S(2)}) copy-start(f32[256,512]{1,0:T(8,128)} %get-tuple-element.169) | copy-start | bytes 1572868
  354.2 64.6 %reduce-scatter.17.cloned.1.call-start = ((), (), s32[]{:S(2)}) async-start(), calls=%async_computation.4 | async-start | bytes 655360
  356.7 4.1 copy-start.111
  356.8 19.2 %copy-start.112 = (u32[32]{0:T(128)S(1)}, u32[32]{0:T(128)}, u32[]{:S(2)}) copy-start(u32[32]{0:T(128)} %constant.124) | copy-start | bytes 388
  358.3 62.3 %copy-start.20 = (bf16[1,512,512]{2,1,0:T(8,128)(2,1)S(1)}, bf16[1,512,512]{2,1,0:T(8,128)(2,1)}, u32[]{:S(2)}) copy-start(bf16[1,512,512]{2,1,0:T(8,128)(2,1)} %copy-done.19) | copy-start | bytes 1572868
  358.3 103.6 %all-reduce.12.cloned.1.call-start = ((), (), s32[]{:S(2)}) async-start(), calls=%async_computation.8 | async-start | bytes 1212416 | tf_op jit(solution)/shard_map/psum | solution.py:169
  370.1 7.0 %collective-permute-start.9 = (bf16[12,512]{1,0:T(8,128)(2,1)S(1)}, bf16[12,512]{1,0:T(8,128)(2,1)S(1)}, u32[]{:S(2)}, u32[]{:S(2)}) collective-permute-start(bf16[12,512]{1,0:T(8,128)(2,1)S(1)} %slice.537), channel_id=1, source_target_pairs={{0,1},{1,2},{2,3},{4,5},{5,6},{6,7},{8,9},{9,10},{10,11},{12,13},{... | collective-permute-start | bytes 36872
  371.6 5.7 %collective-permute-start.8 = (bf16[12,512]{1,0:T(8,128)(2,1)S(1)}, bf16[12,512]{1,0:T(8,128)(2,1)S(1)}, u32[]{:S(2)}, u32[]{:S(2)}) collective-permute-start(bf16[12,512]{1,0:T(8,128)(2,1)S(1)} %slice.536), channel_id=1, source_target_pairs={{0,1},{1,2},{2,3},{4,5},{5,6},{6,7},{8,9},{9,10},{10,11},{12,13},{... | collective-permute-start | bytes 36872
  (85 other events, 170.4 us)
Sparse Core Ops, SparseCore 0:
  246.8 21.4 reduce-scatter.22
  346.0 22.7 reduce-scatter.18
  371.8 22.1 reduce-scatter.20
  397.1 21.6 reduce-scatter.16
  421.8 40.0 all-reduce.11

commit v2 on v0

v2 whole, which is shorter than its diff:
```python
import functools
import math

import jax
import jax.numpy as jnp
from jax import lax
from jax.experimental import pallas as pl
from jax.experimental.pallas import tpu as pltpu
from jax.sharding import PartitionSpec as P

GW = 16
SEC = 256
F32 = jnp.float32
BF16 = jnp.bfloat16
MESH = pl.DeviceIdType.MESH


def bits_of(count):
    return [1 << k for k in range(count.bit_length() - 1)]


def up_to(value, step):
    return -(-value // step) * step


def dot(a, b, contract=((1,), (0,))):
    return lax.dot_general(a, b, (contract, ((), ())), preferred_element_type=F32)


def sigmoid(v):
    return 0.5 + 0.5 * jnp.tanh(0.5 * v)


class Links:
    def __init__(self, send_sems, recv_sems):
        self.send_sems, self.recv_sems = send_sems, recv_sems
        self.used = 0
        self.sent = []

    def copy(self, src, dst, axis, partner):
        k = self.used
        self.used += 1
        made = pltpu.make_async_remote_copy(
            src_ref=src,
            dst_ref=dst,
            send_sem=self.send_sems.at[k],
            recv_sem=self.recv_sems.at[k],
            device_id={axis: partner},
            device_id_type=MESH,
        )
        return made

    def start(self, src, dst, axis, partner):
        made = self.copy(src, dst, axis, partner)
        made.start()
        self.sent.append(made)
        return made


def other(me, bit):
    return me + bit * (1 - 2 * lax.rem(lax.div(me, bit), 2))


def gather_steps(links, buf, axis, me, count):
    for bit in reversed(bits_of(count)):
        copies = []
        for j in range(count // (2 * bit)):
            p = lax.rem(me, 2 * bit) + 2 * bit * j
            copies.append(links.start(buf.at[p], buf.at[p], axis, other(me, bit)))
        yield
        for c in copies:
            c.wait_recv()


def scatter_steps(links, buf, landing, axis, me, count):
    slot = 0
    for bit in bits_of(count):
        b = lax.rem(lax.div(me, bit), 2)
        copies = []
        for j in range(count // (2 * bit)):
            p = lax.rem(me, bit) + bit * (1 - b) + 2 * bit * j
            copies.append(links.start(buf.at[p], landing.at[slot + j], axis, other(me, bit)))
        yield
        for j, c in enumerate(copies):
            c.wait_recv()
            keep = lax.rem(me, bit) + bit * b + 2 * bit * j
            buf[keep] = (buf[keep].astype(F32) + landing[slot + j].astype(F32)).astype(BF16)
        slot += len(copies)


def kernel(n, rows, cols, norm, in_rows, *refs):
    (x_ref, cot_ref, wi_ref, wg_ref, wo_ref, dec_ref, gx_ref, gi_ref, gg_ref, go_ref,
     wi_full, wg_full, wo_full, wg_tmp, wg_flat, k_one, k_two, x3, y3, d1, d2, d3,
     h1, h2, a1, acc, sl3, low, sl2, sl1, halo, e1,
     p_in, p_out, p_group, group_tmp, l_in, l_out, l_group,
     q_in, q_out, q_group, lq_in, lq_out, lq_group, f_in, f_out, f_group,
     send_sems, recv_sems) = refs
    pixels = 2 * cols
    width = x_ref.shape[1]
    sections = width // SEC
    blocks = wi_ref.shape[0]
    grows = wg_ref.shape[1]
    me = lax.axis_index("shard")
    r = lax.axis_index("rows")
    has_up = jnp.where(r > 0, 1, 0)
    has_down = jnp.where(r < rows - 1, 1, 0)
    links = Links(send_sems, recv_sems)

    barrier = pltpu.get_barrier_semaphore()
    for bit in bits_of(n):
        pl.semaphore_signal(barrier, inc=1, device_id={"shard": other(me, bit)}, device_id_type=MESH)
    count = len(bits_of(n))
    if in_rows:
        for bit in bits_of(rows)[1:]:
            pl.semaphore_signal(barrier, inc=1, device_id={"rows": other(r, bit)}, device_id_type=MESH)
            count += 1

    @pl.when(r > 0)
    def _():
        pl.semaphore_signal(barrier, inc=1, device_id={"rows": lax.rem(r + rows - 1, rows)}, device_id_type=MESH)

    @pl.when(r < rows - 1)
    def _():
        pl.semaphore_signal(barrier, inc=1, device_id={"rows": lax.rem(r + 1, rows)}, device_id_type=MESH)

    for b in range(blocks):
        wi_full[b, me] = wi_ref[b]
        wo_full[b, me] = wo_ref[b]
        wg_tmp[...] = jnp.zeros_like(wg_tmp)
        wg_tmp[0:grows, :] = wg_ref[b].astype(F32)
        wg_full[b, me] = wg_tmp[...].astype(BF16)
    pl.semaphore_wait(barrier, count + has_up + has_down)

    gathers = []
    for b in range(blocks):
        for buf in (wi_full, wg_full, wo_full):
            gathers.append(gather_steps(links, buf.at[b], "shard", me, n))
    for g in gathers:
        next(g)

    def finish(g):
        for _ in g:
            pass

    def advance(gens):
        for g in list(gens):
            try:
                next(g)
            except StopIteration:
                gens.remove(g)

    col = lax.broadcasted_iota(jnp.int32, (cols, SEC), 0)
    first, last = col == 0, col == cols - 1
    mask = lax.broadcasted_iota(jnp.int32, (SEC, SEC), 0) // GW == lax.broadcasted_iota(jnp.int32, (SEC, SEC), 1) // GW

    def shifts(v):
        back = jnp.where(first, 0.0, pltpu.roll(v, 1, 0))
        ahead = jnp.where(last, 0.0, pltpu.roll(v, cols - 1, 0))
        return back, ahead

    def put(dst, sec, row, v, flipped):
        back, ahead = shifts(v)
        three = (ahead, v, back) if flipped else (back, v, ahead)
        for k in range(3):
            dst[sec, row * cols:(row + 1) * cols, k * SEC:(k + 1) * SEC] = three[k].astype(BF16)

    def halo_ends(at, src):
        up = pltpu.make_async_remote_copy(
            src_ref=src.at[pl.ds(0, cols)], dst_ref=halo.at[at, 1],
            send_sem=send_sems.at[base + 2 * at], recv_sem=recv_sems.at[base + 2 * at],
            device_id={"rows": lax.rem(r + rows - 1, rows)}, device_id_type=MESH)
        down = pltpu.make_async_remote_copy(
            src_ref=src.at[pl.ds(cols, cols)], dst_ref=halo.at[at, 0],
            send_sem=send_sems.at[base + 2 * at + 1], recv_sem=recv_sems.at[base + 2 * at + 1],
            device_id={"rows": lax.rem(r + 1, rows)}, device_id_type=MESH)
        return up, down

    total_gather = 3 * blocks * (n - 1)
    base = total_gather
    halo_sems = 4 * blocks

    def halo_send(at, src):
        @pl.when(r > 0)
        def _():
            halo_ends(at, src)[0].start()

        @pl.when(r < rows - 1)
        def _():
            halo_ends(at, src)[1].start()

    def halo_wait(at, src):
        @pl.when(r > 0)
        def _():
            up, down = halo_ends(at, src)
            down.wait_recv()
            up.wait_send()

        @pl.when(r == 0)
        def _():
            halo[at, 0] = jnp.zeros((cols, width), BF16)

        @pl.when(r < rows - 1)
        def _():
            up, down = halo_ends(at, src)
            up.wait_recv()
            down.wait_send()

        @pl.when(r == rows - 1)
        def _():
            halo[at, 1] = jnp.zeros((cols, width), BF16)

    def cut(s):
        return slice(s * SEC, (s + 1) * SEC)

    def expand(b):
        for p in range(n):
            wg_flat[p * grows:(p + 1) * grows, :] = wg_full[b, p].astype(F32)[:grows]
        for s in range(sections):
            for tap in range(9):
                dy, dx = tap // 3, tap % 3
                slab = wg_flat[tap * GW:(tap + 1) * GW, cut(s)]
                full = jnp.where(mask, jnp.concatenate([slab] * (SEC // GW), axis=0), 0.0).astype(BF16)
                k_one[b, s, dy, cut(dx), :] = full
                k_two[b, s, dy, :, cut(dx)] = full

    def forward(b, a_ref, out_ref):
        finish(gathers[3 * b])
        for s in range(sections):
            pre = dot(a_ref[...], wi_full[b, :, :, cut(s)].reshape(width, SEC))
            sg = sigmoid(pre)
            hid = pre * sg
            d1[b, :, cut(s)] = sg * (1.0 + pre * (1.0 - sg))
            h1[b, :, cut(s)] = hid.astype(BF16)
        halo_send(b, h1.at[b])
        if b == 0:
            for g in gathers[1:]:
                next(g, None)
        for s in range(sections):
            for row in range(2):
                put(x3.at[b], s, row + 1, h1[b, row * cols:(row + 1) * cols, cut(s)].astype(F32), False)
        finish(gathers[3 * b + 1])
        expand(b)
        for s in range(sections):
            acc[:, cut(s)] = dot(x3[b, s, cols:3 * cols, :], k_one[b, s, 1])
            acc[0:cols, cut(s)] += dot(x3[b, s, 2 * cols:3 * cols, :], k_one[b, s, 2])
            acc[cols:2 * cols, cut(s)] += dot(x3[b, s, cols:2 * cols, :], k_one[b, s, 0])
        halo_wait(b, h1.at[b])
        for s in range(sections):
            for side in range(2):
                put(x3.at[b], s, 3 * side, halo[b, side, :, cut(s)].astype(F32), False)
            top = acc[0:cols, cut(s)] + dot(x3[b, s, 0:cols, :], k_one[b, s, 0])
            low_ = acc[cols:2 * cols, cut(s)] + dot(x3[b, s, 3 * cols:4 * cols, :], k_one[b, s, 2])
            for row, pre in ((0, top), (1, low_)):
                at = slice(row * cols, (row + 1) * cols)
                sg = sigmoid(pre)
                d2[b, at, cut(s)] = sg * (1.0 + pre * (1.0 - sg))
                h2[b, at, cut(s)] = (pre * sg).astype(BF16)
        finish(gathers[3 * b + 2])
        for s in range(sections):
            pre = a_ref[:, cut(s)].astype(F32) + dot(h2[b], wo_full[b, :, :, cut(s)].reshape(width, SEC))
            sg = sigmoid(pre)
            d3[b, :, cut(s)] = sg * (1.0 + pre * (1.0 - sg))
            out_ref[:, cut(s)] = (pre * sg).astype(BF16)

    forward(0, x_ref, a1)
    forward(1, a1, dec_ref)
    links.used = total_gather + halo_sems

    live = []

    def reduce_steps(b, part, landing, q, landing_q, final, out):
        yield from scatter_steps(links, part.at[b], landing.at[b], "shard", me, n)
        if not in_rows:
            out[b] = part[b, me]
            return
        size = part.shape[2] // rows
        total = part[b, me]
        for k in range(rows):
            q[b, k] = total[k * size:(k + 1) * size]
        yield from scatter_steps(links, q.at[b], landing_q.at[b], "rows", r, rows)
        final[b, r] = q[b, r]
        yield from gather_steps(links, final.at[b], "rows", r, rows)
        out[b] = final[b].reshape(part.shape[2], width)[:out.shape[1]].astype(F32) * norm

    def launch(gen):
        live.append(gen)
        advance(live)

    def part_in(b, a_ref):
        for s in range(sections):
            made = dot(a_ref[...], sl1[:, cut(s)], ((0,), (0,))).astype(BF16)
            p_in[b, :, :, cut(s)] = made.reshape(n, width // n, SEC)
        launch(reduce_steps(b, p_in, l_in, q_in, lq_in, f_in, gi_ref))

    def backward(b, e_ref, a_ref, out_ref):
        for s in range(sections):
            v = e_ref[:, cut(s)].astype(F32) * d3[b, :, cut(s)]
            sl3[:, cut(s)] = v
            low[:, cut(s)] = v.astype(BF16)
        for s in range(sections):
            rows_of = wo_full[b].reshape(width, width)[cut(s), :]
            v = dot(low[...], rows_of, ((1,), (1,))) * d2[b, :, cut(s)]
            sl2[b, :, cut(s)] = v.astype(BF16)
        halo_send(blocks + b, sl2.at[b])
        for s in range(sections):
            made = dot(h2[b], low[:, cut(s)], ((0,), (0,))).astype(BF16)
            p_out[b, :, :, cut(s)] = made.reshape(n, width // n, SEC)
        launch(reduce_steps(b, p_out, l_out, q_out, lq_out, f_out, go_ref))
        for s in range(sections):
            for row in range(2):
                put(y3, s, row + 1, sl2[b, row * cols:(row + 1) * cols, cut(s)].astype(F32), True)
        for s in range(sections):
            acc[:, cut(s)] = dot(y3[s, cols:3 * cols, :], k_two[b, s, 1], ((1,), (1,)))
            acc[0:cols, cut(s)] += dot(y3[s, 2 * cols:3 * cols, :], k_two[b, s, 0], ((1,), (1,)))
            acc[cols:2 * cols, cut(s)] += dot(y3[s, cols:2 * cols, :], k_two[b, s, 2], ((1,), (1,)))
        halo_wait(blocks + b, sl2.at[b])
        advance(live)
        for s in range(sections):
            for side in range(2):
                put(y3, s, 3 * side, halo[blocks + b, side, :, cut(s)].astype(F32), True)
            top = acc[0:cols, cut(s)] + dot(y3[s, 0:cols, :], k_two[b, s, 2], ((1,), (1,)))
            low_ = acc[cols:2 * cols, cut(s)] + dot(y3[s, 3 * cols:4 * cols, :], k_two[b, s, 0], ((1,), (1,)))
            for row, back in ((0, top), (1, low_)):
                at = slice(row * cols, (row + 1) * cols)
                sl1[at, cut(s)] = (back * d1[b, at, cut(s)]).astype(BF16)
        part_in(b, a_ref)
        for s in range(sections):
            rows_of = wi_full[b].reshape(width, width)[cut(s), :]
            v = sl3[:, cut(s)] + dot(sl1[...], rows_of, ((1,), (1,)))
            out_ref[:, cut(s)] = v.astype(BF16)
        advance(live)
        for s in range(sections):
            for dy in range(3):
                made = dot(x3[b, s, dy * cols:(dy + 2) * cols, :], sl2[b, :, cut(s)], ((0,), (0,)))
                for dx in range(3):
                    tap = 3 * dy + dx
                    kept = jnp.where(mask, made[cut(dx), :], 0.0)
                    group_tmp[tap * GW:(tap + 1) * GW, cut(s)] = jnp.sum(kept.reshape(SEC // GW, GW, SEC), axis=0)
        gpad = p_group.shape[2]
        for p in range(n):
            p_group[b, p] = group_tmp[p * grows:p * grows + gpad, :].astype(BF16)
        launch(reduce_steps(b, p_group, l_group, q_group, lq_group, f_group, gg_ref))

    group_tmp[...] = jnp.zeros_like(group_tmp)
    backward(1, cot_ref, a1, e1)
    backward(0, e1, x_ref, gx_ref)
    while live:
        advance(live)
    for c in links.sent:
        c.wait_send()


def body(n, rows, images, cotangent, weight_in, weight_group, weight_out):
    tiles, height, cols, width = images.shape
    assert tiles == 1 and height == 2
    pixels = height * cols
    blocks, part, _ = weight_in.shape
    grows = weight_group.shape[1]
    wpad = up_to(grows, 16)
    in_rows = rows == 4 and part % (16 * rows) == 0
    gpad = up_to(grows, 16 * rows) if in_rows else wpad
    sections = width // SEC
    norm = 1.0 / math.sqrt(pixels * rows * n)
    out_type = F32 if in_rows else BF16
    gout = grows if in_rows else gpad
    qn = rows if in_rows else 1
    vm = pltpu.VMEM
    q, gq = part // qn, gpad // qn
    scratch = [
        vm((blocks, n, part, width), BF16), vm((blocks, n, wpad, width), BF16), vm((blocks, n, part, width), BF16),
        vm((wpad, width), F32), vm((up_to(n * grows, 16), width), F32),
        vm((blocks, sections, 3, 3 * SEC, SEC), BF16), vm((blocks, sections, 3, SEC, 3 * SEC), BF16),
        vm((blocks, sections, 4 * cols, 3 * SEC), BF16), vm((sections, 4 * cols, 3 * SEC), BF16),
        vm((blocks, pixels, width), F32), vm((blocks, pixels, width), F32), vm((blocks, pixels, width), F32),
        vm((blocks, pixels, width), BF16), vm((blocks, pixels, width), BF16), vm((pixels, width), BF16),
        vm((pixels, width), F32), vm((pixels, width), F32), vm((pixels, width), BF16),
        vm((blocks, pixels, width), BF16), vm((pixels, width), BF16),
        vm((2 * blocks, 2, cols, width), BF16), vm((pixels, width), BF16),
        vm((blocks, n, part, width), BF16), vm((blocks, n, part, width), BF16), vm((blocks, n, gpad, width), BF16),
        vm((up_to((n - 1) * grows + gpad, 16) + 16, width), F32),
        vm((blocks, n - 1, part, width), BF16), vm((blocks, n - 1, part, width), BF16), vm((blocks, n - 1, gpad, width), BF16),
        vm((blocks, qn, q, width), BF16), vm((blocks, qn, q, width), BF16), vm((blocks, qn, gq, width), BF16),
        vm((blocks, max(qn - 1, 1), q, width), BF16), vm((blocks, max(qn - 1, 1), q, width), BF16), vm((blocks, max(qn - 1, 1), gq, width), BF16),
        vm((blocks, qn, q, width), BF16), vm((blocks, qn, q, width), BF16), vm((blocks, qn, gq, width), BF16),
        pltpu.SemaphoreType.DMA((3 * blocks * (n - 1 + n - 1 + 2 * rows) + 4 * blocks if in_rows else 6 * blocks * (n - 1) + 4 * blocks,)),
        pltpu.SemaphoreType.DMA((3 * blocks * (n - 1 + n - 1 + 2 * rows) + 4 * blocks if in_rows else 6 * blocks * (n - 1) + 4 * blocks,)),
    ]
    spec = pl.BlockSpec(memory_space=pltpu.VMEM)
    dec, gx, gi, gg, go = pl.pallas_call(
        functools.partial(kernel, n, rows, cols, norm, in_rows),
        out_shape=[
            jax.ShapeDtypeStruct((pixels, width), BF16),
            jax.ShapeDtypeStruct((pixels, width), BF16),
            jax.ShapeDtypeStruct((blocks, part, width), out_type),
            jax.ShapeDtypeStruct((blocks, gout, width), out_type),
            jax.ShapeDtypeStruct((blocks, part, width), out_type),
        ],
        in_specs=[spec] * 5,
        out_specs=[spec] * 5,
        scratch_shapes=scratch,
        compiler_params=pltpu.CompilerParams(
            collective_id=0, has_side_effects=True, vmem_limit_bytes=58 * 2**20
        ),
    )(images.reshape(pixels, width), cotangent.reshape(pixels, width), weight_in, weight_group, weight_out)
    if not in_rows:
        gi, gg, go = (lax.psum(v, "rows").astype(F32) * norm for v in (gi, gg[:, :grows], go))
    return dec.reshape(images.shape), gx.reshape(images.shape), gi, gg, go


def solution(mesh):
    tile = P(("groups", "shard"), "rows", None, None)
    weight = P(None, "shard", None)
    grad = P("groups", "shard", None)
    return jax.shard_map(
        functools.partial(body, mesh.shape["shard"], mesh.shape["rows"]),
        mesh=mesh,
        in_specs=(tile, tile, weight, weight, weight),
        out_specs=(tile, tile, grad, grad, grad),
        check_vma=False,
    )
```

time: 442 us -> 93.7 us (0.21); the launches traced: 435 us -> 93.5 us
  local copies, waits for them, and re-layouts: 196 us -> 6.72 us
  Pallas kernels: 0 us -> 86.1 us
  waiting for transfers between devices: 71 us -> 0 us
  blocking collectives: 54.3 us -> 0 us
  matrix products: 44.2 us -> 0 us
  starting transfers between devices: 31.6 us -> 0 us
  other arithmetic: 20.9 us -> 0 us
  between operations: 17.1 us -> 0.66 us
    pallas_call x0 -> x1, Pallas kernels: none -> 86.1 us  [body(): pl.pallas_call(functools.partial(kernel, n, rows, cols, norm, in_rows), o...]
    reshape x94 -> x0, local copies, waits for them, and re-layouts: 74.8 us -> none  [the longest x52 52.9 us: grouped_taps(): window = window.reshape(-1, kernel.shape[1], kernel.shape[2])]
    all_gather x6 -> x0, blocking collectives: 45.6 us -> none  [the longest x2 17.6 us: body(): lax.all_gather(weight_in[block_index], 'shard', axis=0, tiled=True)]
    dot_general x66 -> x0, matrix products: 44.2 us -> none  [the longest x36 16.2 us: grouped_taps(): jnp.einsum(pattern, window, kernel[tap_index], preferred_element_type=jnp...]
    squeeze x18 -> x0, local copies, waits for them, and re-layouts: 42.2 us -> none  [grouped_taps(): kernel[tap_index]]
    psum x1 -> x0, waiting for transfers between devices: 40.3 us -> none  [body(): lax.psum(jnp.stack([entry[0] for entry in shares]).astype(jnp.bfloat16),...]
    unnamed x11 -> x0, waiting for transfers between devices: 30.7 us -> none
    ppermute x8 -> x0, starting transfers between devices: 26.2 us -> none  [the longest x4 21 us: extended_2(): lax.ppermute(tail, axis, [(i, (i + 1) % count) for i in range(ends)])]
  transfers between devices with their start and end apart: 15 -> 0, of which waited for: 3 -> 0; matrix products, arithmetic and copies ran while one was open for 38% -> 0% of each run, Pallas kernels for 0% -> 0%
where the time goes in v2:
time: 93.7 us; the launch traced here: 93.5 us
  Pallas kernels  86.1 us (92%)
  local copies, waits for them, and re-layouts  6.72 us (7%)
    pallas_call x1, Pallas kernels, body(): pl.pallas_call(functools.partial(kernel, n, rows, cols, norm, in_rows), o...  86.1 us
    unnamed x14, local copies, waits for them, and re-layouts  6.72 us

profile of v2, /device:TPU:0, one launch (start us, length us, event | category | flops | bytes accessed | tf_op | source)
XLA Modules:
  0.0 93.5 jit_solution(10687063563446199175)
XLA Ops:
  0.6 1.5 %copy.10.refs_3_ = bf16[2,36,512]{2,1,0:T(8,128)(2,1)} copy(bf16[2,36,512]{2,0,1:T(2,128)(2,1)} %param.8) | data formatting | bytes 147456 | tf_op args[3]
  2.2 86.1 %shard_map.92 = (bf16[256,512]{1,0:T(8,128)(2,1)}, bf16[256,512]{1,0:T(8,128)(2,1)}, f32[2,128,512]{2,1,0:T(8,128)}, f32[2,36,512]{2,1,0:T(8,128)}, f32[2,128,512]{2,1,0:T(8,128)}) custom-call(bf16[256,512]{1,0:T(8,128)(2,1)} %bitcast.4, bf16[256,512]{1,0:T(8,128)(2,1)} %bitcast.5, bf16[2,128,512]{2,1,0:T(8,128)(2,1)} %refs_2_.1, ...), custom_call_target="tpu_custom_call" | custom-call | tf_op jit(solution)/shard_map/pallas_call | solution.py:389
  88.3 0.0 copy-start.3
  88.3 0.0 copy-start.2
  88.3 1.7 %copy.11 = f32[2,36,512]{2,0,1:T(2,128)} copy(f32[2,36,512]{2,1,0:T(8,128)} %get-tuple-element.18) | data formatting | bytes 294912
  90.0 0.0 copy-done.3
  90.0 0.0 copy-start.1
  90.0 0.7 copy.16
  90.7 0.0 copy-done.2
  90.7 0.7 copy.17
  91.5 0.0 copy-done.1
  91.5 0.0 copy-start
  91.5 0.8 copy.18
  92.2 0.4 copy-done
  92.7 0.8 copy.19
Async XLA Ops:
  88.3 1.8 %copy-start.3 = (bf16[256,512]{1,0:T(8,128)(2,1)S(1)}, bf16[256,512]{1,0:T(8,128)(2,1)}, u32[]{:S(2)}) copy-start(bf16[256,512]{1,0:T(8,128)(2,1)} %get-tuple-element.10) | copy-start | bytes 786436
  88.3 2.5 %copy-start.2 = (bf16[256,512]{1,0:T(8,128)(2,1)S(1)}, bf16[256,512]{1,0:T(8,128)(2,1)}, u32[]{:S(2)}) copy-start(bf16[256,512]{1,0:T(8,128)(2,1)} %get-tuple-element.11) | copy-start | bytes 786436
  90.0 1.4 %copy-start.1 = (f32[2,128,512]{2,1,0:T(8,128)S(1)}, f32[2,128,512]{2,1,0:T(8,128)}, u32[]{:S(2)}) copy-start(f32[2,128,512]{2,1,0:T(8,128)} %get-tuple-element.27) | copy-start | bytes 1572868
  91.5 1.2 %copy-start = (f32[2,128,512]{2,1,0:T(8,128)S(1)}, f32[2,128,512]{2,1,0:T(8,128)}, u32[]{:S(2)}) copy-start(f32[2,128,512]{2,1,0:T(8,128)} %get-tuple-element.29) | copy-start | bytes 1572868

commit v3 on v2

--- a/solution.py
+++ b/solution.py
@@ -13,6 +13,7 @@
 F32 = jnp.float32
 BF16 = jnp.bfloat16
 MESH = pl.DeviceIdType.MESH
+STEPS = ((1, 2), (0, 0), (0, 2))
 
 
 def bits_of(count):
@@ -99,7 +100,7 @@
     width = x_ref.shape[1]
     sections = width // SEC
     blocks = wi_ref.shape[0]
-    grows = wg_ref.shape[1]
+    grows = wg_ref.shape[0]
     me = lax.axis_index("shard")
     r = lax.axis_index("rows")
     has_up = jnp.where(r > 0, 1, 0)
@@ -127,7 +128,7 @@
         wi_full[b, me] = wi_ref[b]
         wo_full[b, me] = wo_ref[b]
         wg_tmp[...] = jnp.zeros_like(wg_tmp)
-        wg_tmp[0:grows, :] = wg_ref[b].astype(F32)
+        wg_tmp[0:grows, :] = wg_ref[...].astype(F32)[:, b, :]
         wg_full[b, me] = wg_tmp[...].astype(BF16)
     pl.semaphore_wait(barrier, count + has_up + has_down)
 
@@ -232,13 +233,11 @@
             d1[b, :, cut(s)] = sg * (1.0 + pre * (1.0 - sg))
             h1[b, :, cut(s)] = hid.astype(BF16)
         halo_send(b, h1.at[b])
-        if b == 0:
-            for g in gathers[1:]:
-                next(g, None)
         for s in range(sections):
             for row in range(2):
                 put(x3.at[b], s, row + 1, h1[b, row * cols:(row + 1) * cols, cut(s)].astype(F32), False)
         finish(gathers[3 * b + 1])
+        next(gathers[3 * b + 2], None)
         expand(b)
         for s in range(sections):
             acc[:, cut(s)] = dot(x3[b, s, cols:3 * cols, :], k_one[b, s, 1])
@@ -256,6 +255,8 @@
                 d2[b, at, cut(s)] = sg * (1.0 + pre * (1.0 - sg))
                 h2[b, at, cut(s)] = (pre * sg).astype(BF16)
         finish(gathers[3 * b + 2])
+        if b + 1 < blocks:
+            next(gathers[3 * b + 3], None)
         for s in range(sections):
             pre = a_ref[:, cut(s)].astype(F32) + dot(h2[b], wo_full[b, :, :, cut(s)].reshape(width, SEC))
             sg = sigmoid(pre)
@@ -280,11 +281,19 @@
         yield from scatter_steps(links, q.at[b], landing_q.at[b], "rows", r, rows)
         final[b, r] = q[b, r]
         yield from gather_steps(links, final.at[b], "rows", r, rows)
-        out[b] = final[b].reshape(part.shape[2], width)[:out.shape[1]].astype(F32) * norm
+        done = final[b].reshape(part.shape[2], width).astype(F32) * norm
+        if out is gg_ref:
+            out[:, b, :] = done[:grows]
+        else:
+            out[b] = done
 
     def launch(gen):
+        next(gen)
         live.append(gen)
-        advance(live)
+
+    def step_at(b, at):
+        if (b, at) in STEPS:
+            advance(live)
 
     def part_in(b, a_ref):
         for s in range(sections):
@@ -313,22 +322,7 @@
             acc[:, cut(s)] = dot(y3[s, cols:3 * cols, :], k_two[b, s, 1], ((1,), (1,)))
             acc[0:cols, cut(s)] += dot(y3[s, 2 * cols:3 * cols, :], k_two[b, s, 0], ((1,), (1,)))
             acc[cols:2 * cols, cut(s)] += dot(y3[s, cols:2 * cols, :], k_two[b, s, 2], ((1,), (1,)))
-        halo_wait(blocks + b, sl2.at[b])
-        advance(live)
-        for s in range(sections):
-            for side in range(2):
-                put(y3, s, 3 * side, halo[blocks + b, side, :, cut(s)].astype(F32), True)
-            top = acc[0:cols, cut(s)] + dot(y3[s, 0:cols, :], k_two[b, s, 2], ((1,), (1,)))
-            low_ = acc[cols:2 * cols, cut(s)] + dot(y3[s, 3 * cols:4 * cols, :], k_two[b, s, 0], ((1,), (1,)))
-            for row, back in ((0, top), (1, low_)):
-                at = slice(row * cols, (row + 1) * cols)
-                sl1[at, cut(s)] = (back * d1[b, at, cut(s)]).astype(BF16)
-        part_in(b, a_ref)
-        for s in range(sections):
-            rows_of = wi_full[b].reshape(width, width)[cut(s), :]
-            v = sl3[:, cut(s)] + dot(sl1[...], rows_of, ((1,), (1,)))
-            out_ref[:, cut(s)] = v.astype(BF16)
-        advance(live)
+        step_at(b, 0)
         for s in range(sections):
             for dy in range(3):
                 made = dot(x3[b, s, dy * cols:(dy + 2) * cols, :], sl2[b, :, cut(s)], ((0,), (0,)))
@@ -340,6 +334,27 @@
         for p in range(n):
             p_group[b, p] = group_tmp[p * grows:p * grows + gpad, :].astype(BF16)
         launch(reduce_steps(b, p_group, l_group, q_group, lq_group, f_group, gg_ref))
+        step_at(b, 1)
+        halo_wait(blocks + b, sl2.at[b])
+        step_at(b, 2)
+        for s in range(sections):
+            for side in range(2):
+                put(y3, s, 3 * side, halo[blocks + b, side, :, cut(s)].astype(F32), True)
+            top = acc[0:cols, cut(s)] + dot(y3[s, 0:cols, :], k_two[b, s, 2], ((1,), (1,)))
+            low_ = acc[cols:2 * cols, cut(s)] + dot(y3[s, 3 * cols:4 * cols, :], k_two[b, s, 0], ((1,), (1,)))
+            for row, back in ((0, top), (1, low_)):
+                at = slice(row * cols, (row + 1) * cols)
+                sl1[at, cut(s)] = (back * d1[b, at, cut(s)]).astype(BF16)
+        def flow():
+            for s in range(sections):
+                rows_of = wi_full[b].reshape(width, width)[cut(s), :]
+                v = sl3[:, cut(s)] + dot(sl1[...], rows_of, ((1,), (1,)))
+                out_ref[:, cut(s)] = v.astype(BF16)
+
+        part_in(b, a_ref)
+        step_at(b, 3)
+        flow()
+        step_at(b, 4)
 
     group_tmp[...] = jnp.zeros_like(group_tmp)
     backward(1, cot_ref, a1, e1)
@@ -392,7 +407,7 @@
             jax.ShapeDtypeStruct((pixels, width), BF16),
             jax.ShapeDtypeStruct((pixels, width), BF16),
             jax.ShapeDtypeStruct((blocks, part, width), out_type),
-            jax.ShapeDtypeStruct((blocks, gout, width), out_type),
+            jax.ShapeDtypeStruct((grows, blocks, width) if in_rows else (blocks, gout, width), out_type),
             jax.ShapeDtypeStruct((blocks, part, width), out_type),
         ],
         in_specs=[spec] * 5,
@@ -401,8 +416,10 @@
         compiler_params=pltpu.CompilerParams(
             collective_id=0, has_side_effects=True, vmem_limit_bytes=58 * 2**20
         ),
-    )(images.reshape(pixels, width), cotangent.reshape(pixels, width), weight_in, weight_group, weight_out)
-    if not in_rows:
+    )(images.reshape(pixels, width), cotangent.reshape(pixels, width), weight_in, weight_group.transpose(1, 0, 2), weight_out)
+    if in_rows:
+        gg = gg.transpose(1, 0, 2)
+    else:
         gi, gg, go = (lax.psum(v, "rows").astype(F32) * norm for v in (gi, gg[:, :grows], go))
     return dec.reshape(images.shape), gx.reshape(images.shape), gi, gg, go
 

time: 93.7 us -> 75.5 us (0.81)
  Pallas kernels: 86.1 us -> 69.7 us
  local copies, waits for them, and re-layouts: 6.72 us -> 4.93 us
    pallas_call x1, Pallas kernels: 86.1 us -> 69.7 us  [body(): pl.pallas_call(functools.partial(kernel, n, rows, cols, norm, in_rows), o...]
    unnamed x14 -> x13, local copies, waits for them, and re-layouts: 6.72 us -> 4.93 us
where the time goes in v3:
time: 75.5 us; the launch traced here: 75.3 us
  Pallas kernels  69.7 us (92%)
  local copies, waits for them, and re-layouts  4.93 us (7%)
    pallas_call x1, Pallas kernels, body(): pl.pallas_call(functools.partial(kernel, n, rows, cols, norm, in_rows), o...  69.7 us
    unnamed x13, local copies, waits for them, and re-layouts  4.93 us

profile of v3, /device:TPU:0, one launch (start us, length us, event | category | flops | bytes accessed | tf_op | source)
XLA Modules:
  0.0 75.3 jit_solution(2934826383664324371)
XLA Ops:
  0.6 69.7 %shard_map.92 = (bf16[256,512]{1,0:T(8,128)(2,1)}, bf16[256,512]{1,0:T(8,128)(2,1)}, f32[2,128,512]{2,1,0:T(8,128)}, f32[36,2,512]{2,1,0:T(2,128)}, f32[2,128,512]{2,1,0:T(8,128)}) custom-call(bf16[256,512]{1,0:T(8,128)(2,1)} %bitcast.6, bf16[256,512]{1,0:T(8,128)(2,1)} %bitcast.7, bf16[2,128,512]{2,1,0:T(8,128)(2,1)} %refs_2_.1, ...), custom_call_target="tpu_custom_call" | custom-call | tf_op jit(solution)/shard_map/pallas_call | solution.py:404
  70.3 0.0 copy-start.2
  70.3 0.0 copy-start.1
  70.3 1.7 %copy.15 = bf16[1,2,128,512]{3,2,1,0:T(8,128)(2,1)} copy(bf16[1,2,128,512]{3,2,1,0:T(8,128)(2,1)} %bitcast.9) | data formatting | bytes 524288
  72.1 0.0 copy-done.2
  72.1 0.7 copy.16
  72.8 0.0 copy-done.1
  72.8 0.0 copy-start.3
  72.8 0.0 copy-start
  72.8 0.8 %copy.17 = f32[2,128,512]{2,1,0:T(8,128)} copy(f32[2,128,512]{2,1,0:T(8,128)S(1)} %copy-done.1) | data formatting | bytes 1048576
  73.6 0.2 copy-done.3
  73.8 0.7 copy.18
  74.5 0.0 copy-done
  74.5 0.8 %copy.19 = f32[2,128,512]{2,1,0:T(8,128)} copy(f32[2,128,512]{2,1,0:T(8,128)S(1)} %copy-done) | data formatting | bytes 1048576
Async XLA Ops:
  70.3 1.8 %copy-start.2 = (bf16[256,512]{1,0:T(8,128)(2,1)S(1)}, bf16[256,512]{1,0:T(8,128)(2,1)}, u32[]{:S(2)}) copy-start(bf16[256,512]{1,0:T(8,128)(2,1)} %get-tuple-element.11) | copy-start | bytes 786436
  70.3 2.5 %copy-start.1 = (f32[2,128,512]{2,1,0:T(8,128)S(1)}, f32[2,128,512]{2,1,0:T(8,128)}, u32[]{:S(2)}) copy-start(f32[2,128,512]{2,1,0:T(8,128)} %get-tuple-element.22) | copy-start | bytes 1572868
  72.8 1.0 %copy-start.3 = (f32[36,2,512]{2,1,0:T(2,128)S(1)}, f32[36,2,512]{2,1,0:T(2,128)}, u32[]{:S(2)}) copy-start(f32[36,2,512]{2,1,0:T(2,128)} %get-tuple-element.13) | copy-start | bytes 442372
  72.8 1.7 %copy-start = (f32[2,128,512]{2,1,0:T(8,128)S(1)}, f32[2,128,512]{2,1,0:T(8,128)}, u32[]{:S(2)}) copy-start(f32[2,128,512]{2,1,0:T(8,128)} %get-tuple-element.24) | copy-start | bytes 1572868
